TPU v7x, 32 devices: a whole 2x2x4 slice. The times are simulated.
32 devices in a mesh: section: 4 (over y, x), dp: 8 (over z, core).
Axes of the slice: x: 2, y: 2, z: 4, core: 2. Of those that a mesh axis runs over, the one named last changes fastest.
Arguments:
- inputs: bfloat16 [12288, 512], P('dp'), may hold values from -6 to 6
- weights: bfloat16 [120, 512, 512], P('section')
- biases: float32 [28, 512], P('section'), may hold values from -1.5 to 1.5
- gain_rows: float32 [8, 512], P('section'), may hold values from 0.5 to 1.5
- block_series: int32 [32, 8], P('dp'), may hold values from 0 to 7, as said below
- cotangent: bfloat16 [12288, 512], P('dp'), may hold values from -6 to 6
Outputs:
- layer_output: bfloat16 [12288, 512], P('dp', 'section')
- input_grad: float32 [12288, 512], P('dp', 'section')
- weight_grad: float32 [120, 512, 512], P('section')
- bias_grad: float32 [28, 512], P('section')
- gain_grad: float32 [8, 512], P('section')
Inputs may be any that keep to these rules, and one draw needn't show every extreme that they name: block_series[b, k] numbers the series that holds block k (48 rows) of buffer b, where buffer b is micro-batch b % 4 of device b // 4 along dp: it is 0 for k = 0 and rises by 0 or 1 from one block to the next; every series holds 1 to 4 blocks, some series holds 4 blocks, and in some buffer the number reaches 7.
All inputs are finite; a program needn't handle non-finite values.
Results may differ from a plain program's by a relative error of at most 0.014.
Values may be sent and summed in bfloat16 or wider, within the bound.
No kernel may reach another device: no remote copies, remote signals or barrier semaphores. Data moves between devices by JAX's collectives and lax.ppermute only.
A program may use at most 832 MiB of HBM per device.

v0:
```python
import jax
import jax.numpy as jnp
from jax import lax
from jax.sharding import PartitionSpec as P

D = 512
FF = 2048
SCALE_A = 12
SCALE_B = 16
BLOCK = 48
HALF = 12
TAPS_A = 16
TAPS_B = 12


def shortened(array):

    def short(part):
        return part.astype(jnp.bfloat16) if part.dtype == jnp.float32 else part

    return jax.tree.map(short, array)


def passed_along(value, axis, steps):
    count = lax.axis_size(axis)
    leading, last = (max(0, -steps), min(count, count - steps))
    return lax.ppermute(value, axis, [(source, source + steps) for source in range(leading, last)])


def shift_rows(field_rows, offset, filler):
    if offset == 0:
        return field_rows
    row_count = field_rows.shape[0]
    padding = jnp.full((abs(offset),) + field_rows.shape[1:], filler, field_rows.dtype)
    if offset > 0:
        return jnp.concatenate([field_rows[offset:], padding], 0)
    return jnp.concatenate([padding, field_rows[: row_count + offset]], 0)


def masked_sum(field_rows, series):
    window_sum = jnp.zeros(field_rows.shape, jnp.float32)
    window_count = jnp.zeros((field_rows.shape[0], 1), jnp.float32)
    for offset in range(-HALF, HALF + 1):
        matches = (shift_rows(series, offset, -1) == series)[:, None]
        window_sum = window_sum + jnp.where(matches, shift_rows(field_rows, offset, 0.0), 0.0)
        window_count = window_count + matches.astype(jnp.float32)
    return (window_sum, window_count)


def layer_norm(values, gain_row, shift_row):
    centered = values - jnp.mean(values, axis=-1, keepdims=True)
    variance = jnp.mean(centered * centered, axis=-1, keepdims=True)
    return centered * lax.rsqrt(variance + 1e-05) * gain_row + shift_row


def exact_gelu(values):
    return jax.nn.gelu(values, approximate=False)


def product(left_side, right_side):
    return jnp.dot(left_side, right_side, preferred_element_type=jnp.float32)


def left_product(left_side, right_side):
    return lax.dot_general(
        left_side, right_side, (((0,), (0,)), ((), ())), preferred_element_type=jnp.float32
    )


def right_product(left_side, right_side):
    return lax.dot_general(
        left_side, right_side, (((1,), (1,)), ((), ())), preferred_element_type=jnp.float32
    )


def branch_table():
    return ((SCALE_A, 0, TAPS_A, 0), (SCALE_B, SCALE_A, TAPS_B, TAPS_A))


def blank_state(row_count, channels):
    return jnp.zeros(
        (row_count + row_count // SCALE_A + row_count // SCALE_B, channels), jnp.bfloat16
    )


def pack(stream, first_low, second_low):
    return jnp.concatenate([stream, first_low, second_low], 0)


def unpack(carried, row_count):
    first_end = row_count + row_count // SCALE_A
    return (carried[:row_count], carried[row_count:first_end], carried[first_end:])


def empty_grads(weights, biases, gain_rows):
    return (
        jnp.zeros(weights.shape, jnp.float32),
        jnp.zeros(biases.shape, jnp.float32),
        jnp.zeros(gain_rows.shape, jnp.float32),
    )


def first_of(entry):
    return entry[0]


def stack_tiles(entries, total, channels):
    ordered = sorted(entries, key=first_of)
    pieces = []
    cursor = 0
    for first, tile_block in ordered:
        if first > cursor:
            pieces.append(jnp.zeros((first - cursor, channels, channels), jnp.float32))
        pieces.append(tile_block)
        cursor = first + tile_block.shape[0]
    if cursor < total:
        pieces.append(jnp.zeros((total - cursor, channels, channels), jnp.float32))
    return jnp.concatenate(pieces, 0)


def unfold(coarse, coarse_series, tap_count):
    columns = []
    tap_masks = []
    for offset in range(tap_count):
        matches = (shift_rows(coarse_series, -offset, -1) == coarse_series)[:, None]
        columns.append(
            jnp.where(matches, shift_rows(coarse, -offset, 0.0), jnp.zeros((), coarse.dtype))
        )
        tap_masks.append(matches)
    return (jnp.concatenate(columns, 1), tap_masks)


def season_of(feed_now, series):
    window_sum, window_count = masked_sum(feed_now, series)
    return (
        (feed_now - window_sum / window_count).astype(jnp.bfloat16),
        window_sum / window_count,
        window_count,
    )


def forward_first(weights, biases, gain_rows, series, feed_now, carried):
    row_count, channels = feed_now.shape
    season, trend_part, window_count = season_of(feed_now, series)
    coarse_list = []
    for member, (stride, first_tile, tap_count, tap_first) in enumerate(branch_table()):
        kernel = weights[first_tile : first_tile + stride].reshape(stride * channels, channels)
        pre_act = (
            product(season.reshape(row_count // stride, stride * channels), kernel) + biases[member]
        )
        coarse_list.append(jnp.tanh(pre_act).astype(jnp.bfloat16))
    return (
        pack(season, coarse_list[0], coarse_list[1]),
        jnp.zeros((row_count, channels), jnp.float32),
    )


def forward_second(weights, biases, gain_rows, series, feed_now, carried):
    row_count, channels = feed_now.shape
    pieces = unpack(carried, row_count)
    outgoing = [pieces[0]]
    for member, (stride, first_tile, tap_count, tap_first) in enumerate(branch_table()):
        coarse = pieces[1 + member]
        unfolded, tap_masks = unfold(coarse, series[::stride], tap_count)
        kernel = weights[tap_first : tap_first + tap_count].reshape(tap_count * channels, channels)
        iso_pre = product(unfolded, kernel) + biases[member]
        normed = layer_norm(
            jnp.tanh(iso_pre) + coarse.astype(jnp.float32), gain_rows[member], biases[2 + member]
        )
        outgoing.append(normed.astype(jnp.bfloat16))
    return (
        pack(outgoing[0], outgoing[1], outgoing[2]),
        jnp.zeros((row_count, channels), jnp.float32),
    )


def forward_third(weights, biases, gain_rows, series, feed_now, carried):
    row_count, channels = feed_now.shape
    pieces = unpack(carried, row_count)
    season = pieces[0].astype(jnp.float32)
    merged = biases[4]
    for member, (stride, first_tile, tap_count, tap_first) in enumerate(branch_table()):
        kernel = weights[first_tile : first_tile + stride]
        spread = lax.dot_general(
            pieces[1 + member], kernel, (((1,), (1,)), ((), ())), preferred_element_type=jnp.float32
        ).reshape(row_count, channels)
        upward = layer_norm(
            jnp.tanh(spread + biases[member]) + season, gain_rows[member], biases[2 + member]
        )
        merged = merged + product(upward.astype(jnp.bfloat16), weights[SCALE_A + SCALE_B + member])
    blank_rows = blank_state(row_count, channels)
    return (
        blank_rows.at[:row_count].set(merged.astype(jnp.bfloat16)),
        jnp.zeros((row_count, channels), jnp.float32),
    )


def forward_last(weights, biases, gain_rows, series, feed_now, carried):
    row_count, channels = feed_now.shape
    mixed_rows = unpack(carried, row_count)[0]
    hidden_tiles = FF // D
    hidden_pre = lax.dot_general(
        mixed_rows,
        weights[0:hidden_tiles],
        (((1,), (1,)), ((), ())),
        preferred_element_type=jnp.float32,
    ).reshape(row_count, hidden_tiles * channels) + biases[0:hidden_tiles].reshape(
        hidden_tiles * channels
    )
    activated = exact_gelu(hidden_pre).astype(jnp.bfloat16)
    branch_out = (
        product(
            activated,
            weights[hidden_tiles : 2 * hidden_tiles].reshape(hidden_tiles * channels, channels),
        )
        + biases[hidden_tiles]
    )
    normed = layer_norm(
        mixed_rows.astype(jnp.float32) + branch_out, gain_rows[0], biases[hidden_tiles + 1]
    )
    season, trend_part, window_count = season_of(feed_now, series)
    trend_term = (
        product(trend_part.astype(jnp.bfloat16), weights[2 * hidden_tiles])
        + biases[hidden_tiles + 2]
    )
    return (blank_state(row_count, channels), normed + trend_term)


def forward_spare(weights, biases, gain_rows, series, feed_now, carried):
    row_count, channels = feed_now.shape
    return (blank_state(row_count, channels), jnp.zeros((row_count, channels), jnp.float32))


def backward_first(weights, biases, gain_rows, series, feed_now, target_now, carried, returned):
    row_count, channels = feed_now.shape
    unused_tiles, bias_grads, gain_grads = empty_grads(biases, biases, gain_rows)
    tile_entries = []
    season, trend_part, window_count = season_of(feed_now, series)
    grads_in = unpack(returned, row_count)
    grad_season = grads_in[0].astype(jnp.float32)
    for member, (stride, first_tile, tap_count, tap_first) in enumerate(branch_table()):
        kernel = weights[first_tile : first_tile + stride].reshape(stride * channels, channels)
        blocks = season.reshape(row_count // stride, stride * channels)
        squashed = jnp.tanh(product(blocks, kernel) + biases[member])
        grad_pre = (grads_in[1 + member].astype(jnp.float32) * (1.0 - squashed * squashed)).astype(
            jnp.bfloat16
        )
        tile_entries.append(
            (first_tile, left_product(blocks, grad_pre).reshape(stride, channels, channels))
        )
        bias_grads = bias_grads.at[member].set(jnp.sum(grad_pre.astype(jnp.float32), axis=0))
        grad_season = grad_season + right_product(grad_pre, kernel).reshape(row_count, channels)
    spread_back, unused_count = masked_sum(grad_season / window_count, series)
    tile_grads = stack_tiles(tile_entries, weights.shape[0], channels)
    return (
        blank_state(row_count, channels),
        tile_grads,
        bias_grads,
        gain_grads,
        grad_season - spread_back,
    )


def backward_second(weights, biases, gain_rows, series, feed_now, target_now, carried, returned):
    row_count, channels = feed_now.shape
    unused_tiles, bias_grads, gain_grads = empty_grads(biases, biases, gain_rows)
    tile_entries = []
    pieces = unpack(carried, row_count)
    grads_in = unpack(returned, row_count)
    outgoing = [grads_in[0]]
    for member, (stride, first_tile, tap_count, tap_first) in enumerate(branch_table()):
        coarse = pieces[1 + member]
        unfolded, tap_masks = unfold(coarse, series[::stride], tap_count)
        kernel = weights[tap_first : tap_first + tap_count].reshape(tap_count * channels, channels)
        squashed = jnp.tanh(product(unfolded, kernel) + biases[member])
        normed, pullback = jax.vjp(
            layer_norm, squashed + coarse.astype(jnp.float32), gain_rows[member], biases[2 + member]
        )
        grad_sum, grad_gain, grad_shift = pullback(grads_in[1 + member].astype(jnp.float32))
        grad_iso = (grad_sum * (1.0 - squashed * squashed)).astype(jnp.bfloat16)
        tile_entries.append(
            (tap_first, left_product(unfolded, grad_iso).reshape(tap_count, channels, channels))
        )
        bias_grads = bias_grads.at[member].set(jnp.sum(grad_iso.astype(jnp.float32), axis=0))
        bias_grads = bias_grads.at[2 + member].set(grad_shift)
        gain_grads = gain_grads.at[member].set(grad_gain)
        spread = right_product(grad_iso, kernel).reshape(-1, tap_count, channels)
        grad_coarse = grad_sum
        for offset in range(tap_count):
            grad_coarse = grad_coarse + shift_rows(
                jnp.where(tap_masks[offset], spread[:, offset], 0.0), offset, 0.0
            )
        outgoing.append(grad_coarse.astype(jnp.bfloat16))
    tile_grads = stack_tiles(tile_entries, weights.shape[0], channels)
    return (
        pack(outgoing[0], outgoing[1], outgoing[2]),
        tile_grads,
        bias_grads,
        gain_grads,
        jnp.zeros((row_count, channels), jnp.float32),
    )


def backward_third(weights, biases, gain_rows, series, feed_now, target_now, carried, returned):
    row_count, channels = feed_now.shape
    unused_tiles, bias_grads, gain_grads = empty_grads(biases, biases, gain_rows)
    tile_entries = []
    pieces = unpack(carried, row_count)
    grads_in = unpack(returned, row_count)
    season = pieces[0].astype(jnp.float32)
    grad_mixed = grads_in[0]
    grad_season = jnp.zeros((row_count, channels), jnp.float32)
    outgoing_low = []
    for member, (stride, first_tile, tap_count, tap_first) in enumerate(branch_table()):
        kernel = weights[first_tile : first_tile + stride]
        spread = lax.dot_general(
            pieces[1 + member], kernel, (((1,), (1,)), ((), ())), preferred_element_type=jnp.float32
        ).reshape(row_count, channels)
        squashed = jnp.tanh(spread + biases[member])
        upward, pullback = jax.vjp(
            layer_norm, squashed + season, gain_rows[member], biases[2 + member]
        )
        merge_tile = weights[SCALE_A + SCALE_B + member]
        tile_entries.append(
            (
                SCALE_A + SCALE_B + member,
                left_product(upward.astype(jnp.bfloat16), grad_mixed)[None],
            )
        )
        grad_sum, grad_gain, grad_shift = pullback(right_product(grad_mixed, merge_tile))
        grad_season = grad_season + grad_sum
        grad_upward = (grad_sum * (1.0 - squashed * squashed)).astype(jnp.bfloat16)
        grad_cells = grad_upward.reshape(row_count // stride, stride, channels)
        tile_entries.append(
            (
                first_tile,
                jnp.einsum(
                    "pd,pke->kde",
                    pieces[1 + member],
                    grad_cells,
                    preferred_element_type=jnp.float32,
                ),
            )
        )
        bias_grads = bias_grads.at[member].set(jnp.sum(grad_upward.astype(jnp.float32), axis=0))
        bias_grads = bias_grads.at[2 + member].set(grad_shift)
        gain_grads = gain_grads.at[member].set(grad_gain)
        outgoing_low.append(
            lax.dot_general(
                grad_cells, kernel, (((1, 2), (0, 2)), ((), ())), preferred_element_type=jnp.float32
            ).astype(jnp.bfloat16)
        )
    bias_grads = bias_grads.at[4].set(jnp.sum(grad_mixed.astype(jnp.float32), axis=0))
    tile_grads = stack_tiles(tile_entries, weights.shape[0], channels)
    return (
        pack(grad_season.astype(jnp.bfloat16), outgoing_low[0], outgoing_low[1]),
        tile_grads,
        bias_grads,
        gain_grads,
        jnp.zeros((row_count, channels), jnp.float32),
    )


def backward_last(weights, biases, gain_rows, series, feed_now, target_now, carried, returned):
    row_count, channels = feed_now.shape
    unused_tiles, bias_grads, gain_grads = empty_grads(biases, biases, gain_rows)
    tile_entries = []
    mixed_rows = unpack(carried, row_count)[0]
    hidden_tiles = FF // D
    target_low = target_now.astype(jnp.bfloat16)
    hidden_pre = lax.dot_general(
        mixed_rows,
        weights[0:hidden_tiles],
        (((1,), (1,)), ((), ())),
        preferred_element_type=jnp.float32,
    ).reshape(row_count, hidden_tiles * channels) + biases[0:hidden_tiles].reshape(
        hidden_tiles * channels
    )
    activated_full, gelu_pullback = jax.vjp(exact_gelu, hidden_pre)
    activated = activated_full.astype(jnp.bfloat16)
    output_kernel = weights[hidden_tiles : 2 * hidden_tiles].reshape(
        hidden_tiles * channels, channels
    )
    branch_out = product(activated, output_kernel) + biases[hidden_tiles]
    normed, pullback = jax.vjp(
        layer_norm,
        mixed_rows.astype(jnp.float32) + branch_out,
        gain_rows[0],
        biases[hidden_tiles + 1],
    )
    grad_sum, grad_gain, grad_shift = pullback(target_now)
    grad_branch = grad_sum.astype(jnp.bfloat16)
    tile_entries.append(
        (
            hidden_tiles,
            left_product(activated, grad_branch).reshape(hidden_tiles, channels, channels),
        )
    )
    bias_grads = bias_grads.at[hidden_tiles].set(jnp.sum(grad_branch.astype(jnp.float32), axis=0))
    (grad_hidden,) = gelu_pullback(right_product(grad_branch, output_kernel))
    grad_cells = grad_hidden.astype(jnp.bfloat16).reshape(row_count, hidden_tiles, channels)
    tile_entries.append(
        (0, jnp.einsum("rd,rke->kde", mixed_rows, grad_cells, preferred_element_type=jnp.float32))
    )
    bias_grads = bias_grads.at[0:hidden_tiles].set(jnp.sum(grad_cells.astype(jnp.float32), axis=0))
    grad_mixed = grad_sum + lax.dot_general(
        grad_cells,
        weights[0:hidden_tiles],
        (((1, 2), (0, 2)), ((), ())),
        preferred_element_type=jnp.float32,
    )
    season, trend_part, window_count = season_of(feed_now, series)
    tile_entries.append(
        (2 * hidden_tiles, left_product(trend_part.astype(jnp.bfloat16), target_low)[None])
    )
    bias_grads = bias_grads.at[hidden_tiles + 1].set(grad_shift)
    bias_grads = bias_grads.at[hidden_tiles + 2].set(jnp.sum(target_now, axis=0))
    gain_grads = gain_grads.at[0].set(grad_gain)
    spread_back, unused_count = masked_sum(
        right_product(target_low, weights[2 * hidden_tiles]) / window_count, series
    )
    returning = blank_state(row_count, channels).at[:row_count].set(grad_mixed.astype(jnp.bfloat16))
    tile_grads = stack_tiles(tile_entries, weights.shape[0], channels)
    return (returning, tile_grads, bias_grads, gain_grads, spread_back)


def backward_spare(weights, biases, gain_rows, series, feed_now, target_now, carried, returned):
    row_count, channels = feed_now.shape
    tile_grads, bias_grads, gain_grads = empty_grads(weights, biases, gain_rows)
    return (
        blank_state(row_count, channels),
        tile_grads,
        bias_grads,
        gain_grads,
        jnp.zeros((row_count, channels), jnp.float32),
    )


def shards(inputs, weights, biases, gain_rows, block_series, cotangent):
    section_id = lax.axis_index("section")
    sections = lax.axis_size("section")
    micro_count = block_series.shape[0]
    row_count = inputs.shape[0] // micro_count
    channels = inputs.shape[1]
    feed_rows = inputs.reshape(micro_count, row_count, channels)
    target_rows = cotangent.reshape(micro_count, row_count, channels)
    forward_list = [forward_first, forward_second, forward_third, forward_last, forward_spare]
    backward_list = [backward_first, backward_second, backward_third, backward_last, backward_spare]
    moment_count = micro_count + sections - 1
    carried = blank_state(row_count, channels)
    stored = jnp.zeros((micro_count,) + carried.shape, carried.dtype)
    produced = jnp.zeros((micro_count, row_count, channels), jnp.float32)
    for moment in range(moment_count):
        micro_index = moment - section_id
        active = jnp.logical_and(micro_index >= 0, micro_index < micro_count)
        micro_slot = jnp.clip(micro_index, 0, micro_count - 1)
        series = jnp.repeat(block_series[micro_slot], BLOCK)
        stored = stored.at[micro_slot].set(jnp.where(active, carried, stored[micro_slot]))
        branch = jnp.where(active, section_id, sections)
        outgoing, result = lax.switch(
            branch,
            forward_list,
            weights,
            biases,
            gain_rows,
            series,
            feed_rows[micro_slot].astype(jnp.float32),
            carried,
        )
        produced = produced.at[micro_slot].add(result)
        if moment + 1 < moment_count:
            carried = jax.tree.map(
                lambda part, own: part.astype(own.dtype),
                passed_along(shortened(outgoing), "section", 1),
                outgoing,
            )
    returned = blank_state(row_count, channels)
    input_total = jnp.zeros((micro_count, row_count, channels), jnp.float32)
    grad_sums = None
    for moment in range(moment_count):
        micro_index = moment - (sections - 1 - section_id)
        active = jnp.logical_and(micro_index >= 0, micro_index < micro_count)
        micro_slot = jnp.clip(micro_index, 0, micro_count - 1)
        series = jnp.repeat(block_series[micro_slot], BLOCK)
        branch = jnp.where(active, section_id, sections)
        outgoing, tile_grads, bias_grads, gain_grads, input_part = lax.switch(
            branch,
            backward_list,
            weights,
            biases,
            gain_rows,
            series,
            feed_rows[micro_slot].astype(jnp.float32),
            target_rows[micro_slot].astype(jnp.float32),
            stored[micro_slot],
            returned,
        )
        input_total = input_total.at[micro_slot].add(input_part)
        grad_part = (tile_grads, bias_grads, gain_grads)
        if grad_sums is None:
            grad_sums = grad_part
        else:
            grad_sums = (
                grad_sums[0] + grad_part[0],
                grad_sums[1] + grad_part[1],
                grad_sums[2] + grad_part[2],
            )
        if moment + 1 < moment_count:
            returned = jax.tree.map(
                lambda part, own: part.astype(own.dtype),
                passed_along(shortened(outgoing), "section", -1),
                outgoing,
            )
    grad_sums = lax.psum_scatter(grad_sums, "dp", scatter_dimension=1, tiled=True)
    tile_full, bias_full, gain_full = jax.tree.map(
        lambda part, own: part.astype(own.dtype),
        lax.all_gather(shortened(grad_sums), "dp", axis=1, tiled=True),
        grad_sums,
    )
    share_width = channels // sections
    layer_share, input_share = (
        lax.psum_scatter(
            produced.astype(jnp.bfloat16), "section", scatter_dimension=2, tiled=True
        ).astype(jnp.float32),
        lax.psum_scatter(
            input_total.astype(jnp.bfloat16), "section", scatter_dimension=2, tiled=True
        ).astype(jnp.float32),
    )
    layer_low = layer_share.astype(jnp.bfloat16)
    return (
        layer_low.reshape(micro_count * row_count, share_width),
        input_share.reshape(micro_count * row_count, share_width),
        tile_full,
        bias_full,
        gain_full,
    )


def solution(mesh):
    return jax.shard_map(
        shards,
        mesh=mesh,
        in_specs=(
            P("dp", None),
            P("section", None, None),
            P("section", None),
            P("section", None),
            P("dp", None),
            P("dp", None),
        ),
        out_specs=(
            P("dp", "section"),
            P("dp", "section"),
            P("section", None, None),
            P("section", None),
            P("section", None),
        ),
        check_vma=False,
    )
```

profile of v0, /device:TPU:5, one launch (start us, length us, event | category | flops | bytes accessed | tf_op | source)
XLA Modules:
  0.0 1751.2 jit_solution(11578088768002675251)
XLA Ops:
  37.7 17.7 %conditional.15 = (bf16[440,512]{1,0:T(8,128)(2,1)}, f32[384,512]{1,0:T(8,128)S(1)}) conditional(s32[]{:T(128)} %clamp.43, (s32[384]{0:T(512)S(1)}, f32[384,512]{1,0:T(8,128)S(1)}, bf16[30,512,512]{2,1,0:T(8,128)(2,1)}, f32[7,512]{1,0:T(8,128)S(1)}) %tuple.3774, (bf16[440,512]{1,0:T(8,128)(2,1)S(1)}, ...), branch_computations={%region_17.18_spmd, %region_18.23_spmd, %region_23.28_spmd, %regio... | conditional | flops 1890807936 | bytes 105132736 | solution.py:460
  67.2 35.4 %collective-permute-done.1 = bf16[440,512]{1,0:T(8,128)(2,1)S(1)} collective-permute-done((bf16[440,512]{1,0:T(8,128)(2,1)}, bf16[440,512]{1,0:T(8,128)(2,1)S(1)}, u32[]{:S(2)}, u32[]{:S(2)}) %collective-permute-start.1) | collective-permute-done | bytes 450592 | tf_op jit(solution)/shard_map/ppermute | solution.py:27
  102.7 29.2 %conditional.16 = (bf16[440,512]{1,0:T(8,128)(2,1)}, f32[384,512]{1,0:T(8,128)}) conditional(s32[]{:T(128)} %clamp.44, (s32[384]{0:T(512)S(1)}, f32[384,512]{1,0:T(8,128)}, bf16[30,512,512]{2,1,0:T(8,128)(2,1)}, f32[7,512]{1,0:T(8,128)S(1)}) %tuple.3778, (bf16[440,512]{1,0:T(8,128)(2,1)S(1)}, s32[384]{0:T(512)S(1)}, ...), branch_computations={%region_33.34_spmd, %region_34.39_spmd, %region_39.44_spmd, %regio... | conditional | flops 1890807936 | bytes 111424288 | solution.py:460
  146.4 29.0 %conditional.17 = (bf16[440,512]{1,0:T(8,128)(2,1)}, f32[384,512]{1,0:T(8,128)}) conditional(s32[]{:T(128)} %clamp.45, (s32[384]{0:T(512)S(1)}, f32[384,512]{1,0:T(8,128)}, bf16[30,512,512]{2,1,0:T(8,128)(2,1)}, f32[7,512]{1,0:T(8,128)S(1)}) %tuple.3782, (bf16[440,512]{1,0:T(8,128)(2,1)S(1)}, s32[384]{0:T(512)S(1)}, ...), branch_computations={%region_49.50_spmd, %region_50.55_spmd, %region_55.60_spmd, %regio... | conditional | flops 1890807936 | bytes 111424288 | solution.py:460
  194.8 28.3 %conditional.18 = (bf16[440,512]{1,0:T(8,128)(2,1)S(1)}, f32[384,512]{1,0:T(8,128)}) conditional(s32[]{:T(128)} %clamp.46, (s32[384]{0:T(512)S(1)}, f32[384,512]{1,0:T(8,128)S(1)}, bf16[30,512,512]{2,1,0:T(8,128)(2,1)}, f32[7,512]{1,0:T(8,128)S(1)}) %tuple.3829, (bf16[440,512]{1,0:T(8,128)(2,1)S(1)}, ...), branch_computations={%region_65.66_spmd, %region_66.71_spmd, %region_71.76_spmd, %regio... | conditional | flops 1890807936 | bytes 108278528 | solution.py:460
  223.1 13.5 collective-permute-start.4
  243.5 27.7 %conditional.19 = (bf16[440,512]{1,0:T(8,128)(2,1)S(1)}, f32[384,512]{1,0:T(8,128)}) conditional(s32[]{:T(128)} %clamp.47, (s32[384]{0:T(512)S(1)}, f32[384,512]{1,0:T(8,128)S(1)}, bf16[30,512,512]{2,1,0:T(8,128)(2,1)}, f32[7,512]{1,0:T(8,128)S(1)}) %tuple.3826, (bf16[440,512]{1,0:T(8,128)(2,1)S(1)}, ...), branch_computations={%region_81.82_spmd, %region_82.87_spmd, %region_87.92_spmd, %regio... | conditional | flops 1890807936 | bytes 106705632 | solution.py:460
  296.0 42.5 %conditional.21 = (bf16[440,512]{1,0:T(8,128)(2,1)}, f32[30,512,512]{2,1,0:T(8,128)}, f32[7,512]{1,0:T(8,128)}, f32[2,512]{1,0:T(2,128)S(1)}, f32[1,384,512]{2,1,0:T(8,128)}) conditional(s32[]{:T(128)} %clamp.49, (s32[384]{0:T(512)S(1)}, f32[384,512]{1,0:T(8,128)S(1)}, bf16[30,512,512]{2,1,0:T(8,128)(2,1)}, ...), branch_computations={%region_106.109_spmd, %region_109.122_spmd, %region_122.137_spmd, ... | conditional | flops 5412252672 | bytes 315467744 | solution.py:486
  322.9 15.0 broadcast.11850
  341.2 71.7 %collective-permute-done.6 = bf16[440,512]{1,0:T(8,128)(2,1)S(1)} collective-permute-done((bf16[440,512]{1,0:T(8,128)(2,1)}, bf16[440,512]{1,0:T(8,128)(2,1)S(1)}, u32[]{:S(2)}, u32[]{:S(2)}) %collective-permute-start.6) | collective-permute-done | bytes 450592 | tf_op jit(solution)/shard_map/ppermute | solution.py:27
  412.9 106.7 %conditional.22 = (bf16[440,512]{1,0:T(8,128)(2,1)}, f32[30,512,512]{2,1,0:T(8,128)}, f32[7,512]{1,0:T(8,128)}, f32[2,512]{1,0:T(2,128)S(1)}, f32[1,384,512]{2,1,0:T(8,128)}) conditional(s32[]{:T(128)} %clamp.50, (s32[384]{0:T(512)S(1)}, f32[384,512]{1,0:T(8,128)}, bf16[440,512]{1,0:T(8,128)(2,1)S(1)}, ...), branch_computations={%region_148.151_spmd, %region_151.166_spmd, %region_166.182_spmd, ... | conditional | flops 5412252672 | bytes 318690432 | solution.py:486
  473.1 30.7 %copy.798 = f32[30,512,512]{2,1,0:T(8,128)} copy(f32[30,512,512]{1,2,0:T(8,128)} %pad_maximum_fusion.19) | data formatting | bytes 62914560 | tf_op jit(solution)/shard_map
  528.9 106.6 %conditional.23 = (bf16[440,512]{1,0:T(8,128)(2,1)}, f32[30,512,512]{2,1,0:T(8,128)}, f32[7,512]{1,0:T(8,128)}, f32[2,512]{1,0:T(2,128)S(1)}, f32[1,384,512]{2,1,0:T(8,128)}) conditional(s32[]{:T(128)} %clamp.51, (s32[384]{0:T(512)S(1)}, f32[384,512]{1,0:T(8,128)}, bf16[440,512]{1,0:T(8,128)(2,1)S(1)}, ...), branch_computations={%region_193.196_spmd, %region_196.211_spmd, %region_211.227_spmd, ... | conditional | flops 5412252672 | bytes 318690432 | solution.py:486
  589.1 30.7 %copy.815 = f32[30,512,512]{2,1,0:T(8,128)} copy(f32[30,512,512]{1,2,0:T(8,128)} %pad_maximum_fusion.24) | data formatting | bytes 62914560 | tf_op jit(solution)/shard_map
  644.9 106.7 %conditional.24 = (bf16[440,512]{1,0:T(8,128)(2,1)}, f32[30,512,512]{2,1,0:T(8,128)}, f32[7,512]{1,0:T(8,128)}, f32[2,512]{1,0:T(2,128)S(1)}, f32[1,384,512]{2,1,0:T(8,128)}) conditional(s32[]{:T(128)} %clamp.52, (s32[384]{0:T(512)S(1)}, f32[384,512]{1,0:T(8,128)}, bf16[440,512]{1,0:T(8,128)(2,1)S(1)}, ...), branch_computations={%region_238.241_spmd, %region_241.256_spmd, %region_256.272_spmd, ... | conditional | flops 5412252672 | bytes 318690432 | solution.py:486
  705.2 30.7 %copy.832 = f32[30,512,512]{2,1,0:T(8,128)} copy(f32[30,512,512]{1,2,0:T(8,128)} %pad_maximum_fusion.29) | data formatting | bytes 62914560 | tf_op jit(solution)/shard_map
  760.9 106.6 %conditional.25 = (bf16[440,512]{1,0:T(8,128)(2,1)}, f32[30,512,512]{2,1,0:T(8,128)}, f32[7,512]{1,0:T(8,128)}, f32[2,512]{1,0:T(2,128)S(1)}, f32[1,384,512]{2,1,0:T(8,128)}) conditional(s32[]{:T(128)} %clamp.53, (s32[384]{0:T(512)S(1)}, f32[384,512]{1,0:T(8,128)}, bf16[440,512]{1,0:T(8,128)(2,1)S(1)}, ...), branch_computations={%region_283.286_spmd, %region_286.301_spmd, %region_301.317_spmd, ... | conditional | flops 5412252672 | bytes 318690432 | solution.py:486
  821.1 30.7 %copy.849 = f32[30,512,512]{2,1,0:T(8,128)} copy(f32[30,512,512]{1,2,0:T(8,128)} %pad_maximum_fusion.34) | data formatting | bytes 62914560 | tf_op jit(solution)/shard_map
  876.9 41.7 %conditional.26 = (bf16[440,512]{1,0:T(8,128)(2,1)}, f32[30,512,512]{2,1,0:T(8,128)}, f32[7,512]{1,0:T(8,128)}, f32[2,512]{1,0:T(2,128)S(1)}, f32[1,384,512]{2,1,0:T(8,128)}) conditional(s32[]{:T(128)} %clamp.54, (s32[384]{0:T(512)S(1)}, f32[384,512]{1,0:T(8,128)}, bf16[440,512]{1,0:T(8,128)(2,1)S(1)}, ...), branch_computations={%region_328.331_spmd, %region_331.346_spmd, %region_346.362_spmd, ... | conditional | flops 5412252672 | bytes 324981984 | solution.py:486
  903.9 14.4 broadcast.14529
  918.6 55.0 %collective-permute-start.11 = (bf16[440,512]{1,0:T(8,128)(2,1)}, bf16[440,512]{1,0:T(8,128)(2,1)S(1)}, u32[]{:S(2)}, u32[]{:S(2)}) collective-permute-start(bf16[440,512]{1,0:T(8,128)(2,1)} %get-tuple-element.3199), channel_id=1, source_target_pairs={{8,0},{16,8},{24,16},{9,1},{17,9},{25,17},{10,2},{18,10},{26,18},{... | collective-permute-start | bytes 1351688 | tf_op jit(solution)/shard_map/ppermute | solution.py:27
  979.3 37.3 %conditional.27 = (f32[30,512,512]{2,1,0:T(8,128)}, f32[7,512]{1,0:T(8,128)}, f32[2,512]{1,0:T(2,128)S(1)}, f32[1,384,512]{2,1,0:T(8,128)}) conditional(s32[]{:T(128)} %clamp.55, (s32[384]{0:T(512)S(1)}, f32[384,512]{1,0:T(8,128)S(1)}, bf16[440,512]{1,0:T(8,128)(2,1)S(1)}, bf16[30,512,512]{2,1,0:T(8,128)(2,1)}, ...), branch_computations={%region_373.376_spmd, %region_376.391_spmd, %region_391.407_spmd, ... | conditional | flops 4606356480 | bytes 308802592 | solution.py:486
  1002.0 14.4 broadcast.15009
  1016.6 79.4 %add_add_fusion.41 = f32[30,512,512]{2,1,0:T(8,128)} fusion(f32[30,512,512]{2,1,0:T(8,128)} %get-tuple-element.3207, f32[30,512,512]{2,1,0:T(8,128)} %get-tuple-element.3206, f32[30,512,512]{2,1,0:T(8,128)} %get-tuple-element.3205, f32[30,512,512]{2,1,0:T(8,128)} %get-tuple-element.3204, f32[30,512,512]{2,1,0:T(8,128)} %get-tuple-element.3203, ...), kind=kLoop, calls=%fused_computation.4706 | loop fusion | flops 47185920 | bytes 251658240 | tf_op jit(solution)/shard_map/add | solution.py:504
  1142.2 308.3 %reduce-scatter.14.cloned.1.call-done = f32[30,64,512]{2,1,0:T(8,128)} async-done(((f32[30,512,512]{2,1,0:T(8,128)}), f32[30,64,512]{2,1,0:T(8,128)}) %reduce-scatter.14.cloned.1.call-update) | async-done | bytes 3932176 | tf_op jit(solution)/shard_map/reduce_scatter | solution.py:514
  1454.2 26.3 %reduce-scatter.22.cloned.1.call-done = f32[64,2]{1,0:T(8,128)} async-done(((f32[512,2]{1,0:T(8,128)}), f32[64,2]{1,0:T(8,128)}) %reduce-scatter.22.cloned.1.call-update) | async-done | bytes 528
  1494.0 18.0 %reduce-scatter.20.cloned.1.call-done = f32[64,7]{1,0:T(8,128)} async-done(((f32[512,7]{1,0:T(8,128)}), f32[64,7]{1,0:T(8,128)}) %reduce-scatter.20.cloned.1.call-update) | async-done | bytes 1808
  1512.8 16.4 all-gather
  1529.8 17.2 reduce-scatter.16.cloned.1.call-done
  1549.1 31.7 %reduce-scatter.18.cloned.1.call-done = bf16[128,1536]{1,0:T(8,128)(2,1)} async-done(((bf16[512,1536]{1,0:T(8,128)(2,1)}), bf16[128,1536]{1,0:T(8,128)(2,1)}) %reduce-scatter.18.cloned.1.call-update) | async-done | bytes 393232
  1583.1 142.7 %all-gather.4.cloned.1.call-done = bf16[30,512,512]{2,1,0:T(8,128)(2,1)} async-done(((bf16[30,64,512]{2,1,0:T(8,128)(2,1)}), bf16[30,512,512]{2,1,0:T(8,128)(2,1)}) %all-gather.4.cloned.1.call-update) | async-done | bytes 15728656 | tf_op jit(solution)/shard_map/all_gather | solution.py:517
  1725.8 17.9 %convert_element_type.4121 = f32[30,512,512]{2,1,0:T(8,128)} convert(bf16[30,512,512]{2,1,0:T(8,128)(2,1)} %all-gather.4.cloned.1.call-done) | non-fusion elementwise | flops 7864320 | bytes 47185920 | tf_op jit(solution)/shard_map/convert_element_type | solution.py:516
  (506 shorter events, 540.5 us)
Async XLA Ops:
  7.2 1443.3 %reduce-scatter.14.cloned.1.call-start = ((), (), s32[]{:S(2)}) async-start(), calls=%async_computation.5 | async-start | bytes 35389440 | tf_op jit(solution)/shard_map/reduce_scatter | solution.py:514
  23.5 14.2 collective-permute-start
  56.3 46.3 %collective-permute-start.1 = (bf16[440,512]{1,0:T(8,128)(2,1)}, bf16[440,512]{1,0:T(8,128)(2,1)S(1)}, u32[]{:S(2)}, u32[]{:S(2)}) collective-permute-start(bf16[440,512]{1,0:T(8,128)(2,1)} %get-tuple-element.3179), channel_id=1, source_target_pairs={{0,8},{8,16},{16,24},{1,9},{9,17},{17,25},{2,10},{10,18},{18,26},{... | collective-permute-start | bytes 1351688 | tf_op jit(solution)/shard_map/ppermute | solution.py:27
  131.8 14.6 collective-permute-start.2
  175.4 19.3 %copy-start.14 = (f32[384,512]{1,0:T(8,128)S(1)}, f32[384,512]{1,0:T(8,128)}, u32[]{:S(2)}) copy-start(f32[384,512]{1,0:T(8,128)} %get-tuple-element.7243) | copy-start | bytes 2359300
  175.5 19.3 %copy-start.103 = (s32[384]{0:T(512)S(1)}, s32[384]{0:T(512)}, u32[]{:S(2)}) copy-start(s32[384]{0:T(512)} %reshape.9134) | copy-start | bytes 4612
  175.5 19.3 %collective-permute-start.3 = (bf16[440,512]{1,0:T(8,128)(2,1)}, bf16[440,512]{1,0:T(8,128)(2,1)S(1)}, u32[]{:S(2)}, u32[]{:S(2)}) collective-permute-start(bf16[440,512]{1,0:T(8,128)(2,1)} %get-tuple-element.3183), channel_id=1, source_target_pairs={{0,8},{8,16},{16,24},{1,9},{9,17},{17,25},{2,10},{10,18},{18,26},{... | collective-permute-start | bytes 1351688 | tf_op jit(solution)/shard_map/ppermute | solution.py:27
  223.1 20.4 %copy-start.13 = (f32[384,512]{1,0:T(8,128)S(1)}, f32[384,512]{1,0:T(8,128)}, u32[]{:S(2)}) copy-start(f32[384,512]{1,0:T(8,128)} %get-tuple-element.7242) | copy-start | bytes 2359300
  223.1 20.4 %copy-start.102 = (s32[384]{0:T(512)S(1)}, s32[384]{0:T(512)}, u32[]{:S(2)}) copy-start(s32[384]{0:T(512)} %reshape.9136) | copy-start | bytes 4612
  223.1 20.4 %collective-permute-start.4 = (bf16[440,512]{1,0:T(8,128)(2,1)S(1)}, bf16[440,512]{1,0:T(8,128)(2,1)S(1)}, u32[]{:S(2)}, u32[]{:S(2)}) collective-permute-start(bf16[440,512]{1,0:T(8,128)(2,1)S(1)} %get-tuple-element.3185), channel_id=1, source_target_pairs={{0,8},{8,16},{16,24},{1,9},{9,17},{17,25},{2,10},{10,18},{18,26},{... | collective-permute-start | bytes 1351688 | tf_op jit(solution)/shard_map/ppermute | solution.py:27
  271.9 19.7 %collective-permute-start.5 = (bf16[440,512]{1,0:T(8,128)(2,1)}, bf16[440,512]{1,0:T(8,128)(2,1)S(1)}, u32[]{:S(2)}, u32[]{:S(2)}) collective-permute-start(bf16[440,512]{1,0:T(8,128)(2,1)} %copy-done.203), channel_id=1, source_target_pairs={{0,8},{8,16},{16,24},{1,9},{9,17},{17,25},{2,10},{10,18},{18,26},{... | collective-permute-start | bytes 1351688 | tf_op jit(solution)/shard_map/ppermute | solution.py:27
  338.5 74.4 %copy-start.239 = (f32[2,512]{1,0:T(2,128)}, f32[2,512]{1,0:T(2,128)S(1)}, u32[]{:S(2)}) copy-start(f32[2,512]{1,0:T(2,128)S(1)} %get-tuple-element.3215) | copy-start | bytes 12292
  338.5 74.4 %collective-permute-start.6 = (bf16[440,512]{1,0:T(8,128)(2,1)}, bf16[440,512]{1,0:T(8,128)(2,1)S(1)}, u32[]{:S(2)}, u32[]{:S(2)}) collective-permute-start(bf16[440,512]{1,0:T(8,128)(2,1)} %get-tuple-element.3189), channel_id=1, source_target_pairs={{8,0},{16,8},{24,16},{9,1},{17,9},{25,17},{10,2},{18,10},{26,18},{... | collective-permute-start | bytes 1351688 | tf_op jit(solution)/shard_map/ppermute | solution.py:27
  519.6 9.4 copy-start.241
  519.6 9.3 collective-permute-start.7
  635.5 9.4 copy-start.243
  635.5 9.3 collective-permute-start.8
  751.6 9.4 copy-start.245
  751.6 9.3 collective-permute-start.9
  867.5 9.4 copy-start.247
  867.5 9.3 collective-permute-start.10
  876.9 102.4 %copy-start = (f32[384,512]{1,0:T(8,128)S(1)}, f32[384,512]{1,0:T(8,128)}, u32[]{:S(2)}) copy-start(f32[384,512]{1,0:T(8,128)} %get-tuple-element.7235) | copy-start | bytes 2359300
  876.9 102.4 %copy-start.43 = (bf16[440,512]{1,0:T(8,128)(2,1)S(1)}, bf16[440,512]{1,0:T(8,128)(2,1)}, u32[]{:S(2)}) copy-start(bf16[440,512]{1,0:T(8,128)(2,1)} %get-tuple-element.7228) | copy-start | bytes 1351684
  918.6 60.7 %copy-start.249 = (f32[2,512]{1,0:T(2,128)}, f32[2,512]{1,0:T(2,128)S(1)}, u32[]{:S(2)}) copy-start(f32[2,512]{1,0:T(2,128)S(1)} %get-tuple-element.3220) | copy-start | bytes 12292
  918.6 60.7 %collective-permute-start.11 = (bf16[440,512]{1,0:T(8,128)(2,1)}, bf16[440,512]{1,0:T(8,128)(2,1)S(1)}, u32[]{:S(2)}, u32[]{:S(2)}) collective-permute-start(bf16[440,512]{1,0:T(8,128)(2,1)} %get-tuple-element.3199), channel_id=1, source_target_pairs={{8,0},{16,8},{24,16},{9,1},{17,9},{25,17},{10,2},{18,10},{26,18},{... | collective-permute-start | bytes 1351688 | tf_op jit(solution)/shard_map/ppermute | solution.py:27
  1096.1 384.4 %reduce-scatter.22.cloned.1.call-start = ((), (), s32[]{:S(2)}) async-start(), calls=%async_computation.10 | async-start | bytes 294912
  1108.2 7.2 copy-start.208
  1108.2 7.2 copy-start.213
  1115.3 396.6 %reduce-scatter.20.cloned.1.call-start = ((), (), s32[]{:S(2)}) async-start(), calls=%async_computation.9 | async-start | bytes 294912
  1116.4 430.6 %reduce-scatter.16.cloned.1.call-start = ((), (), s32[]{:S(2)}) async-start(), calls=%async_computation.7 | async-start | bytes 1966080
  1124.3 456.5 %reduce-scatter.18.cloned.1.call-start = ((), (), s32[]{:S(2)}) async-start(), calls=%async_computation.8 | async-start | bytes 1966080
  1142.2 583.7 %all-gather.4.cloned.1.call-start = ((), (), s32[]{:S(2)}) async-start(), calls=%async_computation.6 | async-start | bytes 17694720 | tf_op jit(solution)/shard_map/all_gather | solution.py:517
  (57 other events, 215.3 us)
Sparse Core Ops, SparseCore 0:
  1096.2 354.2 reduce-scatter.13
  1452.7 27.6 reduce-scatter.21
  1483.4 28.5 reduce-scatter.19
  1514.8 32.1 reduce-scatter.15
  1549.8 30.8 reduce-scatter.17
  1582.8 142.9 all-gather.3
where the time goes:
time: 1770 us; the launch traced here: 1750 us
  waiting for transfers between devices  720 us (41%)
  local copies, waits for them, and re-layouts  269 us (15%)
  other arithmetic  234 us (13%)
  loops' own time  208 us (12%)
  matrix products  166 us (9%)
  starting transfers between devices  110 us (6%)
  blocking collectives  28.4 us (2%)
    reduce_scatter x1, waiting for transfers between devices, shards(): lax.psum_scatter(grad_sums, 'dp', scatter_dimension=1, tiled=True)  308 us
    another operation x32, local copies, waits for them, and re-layouts  184 us
    ppermute x12, waiting for transfers between devices, passed_along(): lax.ppermute(value, axis, [(source, source + steps) for source in range(l...  176 us
    another operation x7, loops' own time, shards(): lax.switch(branch, backward_list, weights, biases, gain_rows, series, fee...  152 us
    all_gather x1, waiting for transfers between devices, shards(): lax.all_gather(shortened(grad_sums), 'dp', axis=1, tiled=True)  143 us
    ppermute x12, starting transfers between devices, passed_along(): lax.ppermute(value, axis, [(source, source + steps) for source in range(l...  110 us
    unnamed x10, waiting for transfers between devices  93.2 us
    add x1, other arithmetic, shards(): grad_sums[0] + grad_part[0]  79.4 us
  transfers between devices with their start and end apart: 18, of which 18 were waited for; matrix products, arithmetic and copies ran while one was open for 4% of the time, Pallas kernels for 0%

commit v1 on v0

v1 whole, which is shorter than its diff:
```python
import math

import jax
import jax.numpy as jnp
from jax import lax
from jax.experimental import pallas as pl
from jax.experimental.pallas import tpu as pltpu
from jax.sharding import PartitionSpec as P

D = 512
HIDDEN_TILES = 4
SCALE_A = 12
SCALE_B = 16
BLOCK = 48
HALF = 12
TAPS_A = 16
TAPS_B = 12
DOWN_TILES = SCALE_A + SCALE_B
SMALL_ROWS = 16
LANES = 128
COLS = D // LANES

F32 = jnp.float32
BF16 = jnp.bfloat16

STRIDES = (SCALE_A, SCALE_B)
FIRST_TILE = (0, SCALE_A)
TAPS = (TAPS_A, TAPS_B)
FIRST_TAP = (0, TAPS_A)


def mm(a, b):
    return jnp.dot(a, b, preferred_element_type=F32)


def mm_nt(a, b):
    return lax.dot_general(a, b, (((1,), (1,)), ((), ())), preferred_element_type=F32)


def mm_tn(a, b):
    return lax.dot_general(a, b, (((0,), (0,)), ((), ())), preferred_element_type=F32)


def row_mean(v):
    return jnp.mean(v, axis=-1, keepdims=True)


def col_sum(v):
    return jnp.sum(v, axis=0, keepdims=True)


def normal(v):
    centered = v - row_mean(v)
    scale = lax.rsqrt(row_mean(centered * centered) + 1e-05)
    return centered * scale, scale


def normal_back(o, gain, n, scale):
    og = o * gain
    return scale * (og - row_mean(og) - n * row_mean(og * n))


def spread_get(ref, lead, start, size, stride):
    return jnp.concatenate(
        [ref[lead + (c, pl.ds(start, size, stride=stride), slice(None))] for c in range(COLS)], 1
    )


def spread_set(ref, lead, start, size, stride, value):
    for c in range(COLS):
        ref[lead + (c, pl.ds(start, size, stride=stride), slice(None))] = value[
            :, c * LANES : (c + 1) * LANES
        ]


def block_get(ref, lead, start, size):
    return jnp.concatenate(
        [ref[lead + (c, pl.ds(start, size), slice(None))] for c in range(COLS)], 1
    )


def block_set(ref, lead, start, size, value):
    for c in range(COLS):
        ref[lead + (c, pl.ds(start, size), slice(None))] = value[:, c * LANES : (c + 1) * LANES]


def window_of(col, row):
    size = col.shape[0]
    at = lax.broadcasted_iota(jnp.int32, (size, size), 0)
    to = lax.broadcasted_iota(jnp.int32, (size, size), 1)
    hit = jnp.logical_and(jnp.abs(at - to) <= HALF, col == row)
    ones = jnp.where(hit, 1.0, 0.0).astype(F32)
    return ones.astype(BF16), jnp.sum(ones, axis=1, keepdims=True)


def call(body, name, ins, outs, scratch, flops=0, moved=0, aliases=None, limit=58):
    spaces = {"v": pltpu.VMEM, "a": pl.ANY, "s": pltpu.SMEM}
    return pl.pallas_call(
        body,
        name=name,
        out_shape=[jax.ShapeDtypeStruct(shape, kind) for shape, kind, _ in outs],
        in_specs=[pl.BlockSpec(memory_space=spaces[place]) for _, place in ins],
        out_specs=[pl.BlockSpec(memory_space=spaces[place]) for _, _, place in outs],
        scratch_shapes=scratch,
        input_output_aliases=aliases or {},
        cost_estimate=pl.CostEstimate(flops=flops, bytes_accessed=moved, transcendentals=0),
        compiler_params=pltpu.CompilerParams(vmem_limit_bytes=limit << 20),
    )(*[array for array, _ in ins])


def sems(count):
    return pltpu.SemaphoreType.DMA((count,))


class Copies:
    def __init__(self, ref):
        self.ref = ref
        self.used = 0

    def go(self, source, target):
        copy = pltpu.make_async_copy(source, target, self.ref.at[self.used])
        self.used += 1
        copy.start()
        return copy


def all_wait(copies):
    for copy in copies:
        copy.wait()


def season_body(sid, x, sc, sr, bias, w, season, down, squash, cb, wbuf, sem):
    first = sid[0] == 0
    rows = sr.shape[1]
    buffers = sr.shape[0]

    def tile_copy(k):
        return pltpu.make_async_copy(w.at[k], wbuf.at[k], sem.at[k])

    @pl.when(first)
    def _():
        for k in range(DOWN_TILES):
            tile_copy(k).start()

    for m in range(buffers):
        span = slice(m * rows, (m + 1) * rows)
        ones, count = window_of(sc[span, :], sr[m : m + 1, :])
        feed = x[span, :]
        low = (feed.astype(F32) - mm(ones, feed) / count).astype(BF16)
        season[span, :] = low
        block_set(cb, (), m * rows, rows, low.astype(F32))

    @pl.when(first)
    def _():
        at = 0
        for member in range(2):
            stride = STRIDES[member]
            spots = buffers * rows // stride
            total = jnp.zeros((spots, D), F32)
            for k in range(stride):
                tile = FIRST_TILE[member] + k
                tile_copy(tile).wait()
                total += mm(spread_get(cb, (), k, spots, stride).astype(BF16), wbuf[tile])
            flat = jnp.tanh(total + bias[member : member + 1, :])
            squash[at : at + spots, :] = flat
            down[at : at + spots, :] = flat.astype(BF16)
            at += spots


def trend_body(sid, x, cot, sc, sr, bias, w, tp, ig, dw, xv, gv, tpv, igv, dwv, wv, sem):
    rows = sr.shape[1]
    buffers = sr.shape[0]

    @pl.when(sid[0] == 3)
    def _():
        go = Copies(sem)
        all_wait([go.go(x, xv), go.go(cot, gv), go.go(w.at[2 * HIDDEN_TILES], wv)])
        total = jnp.zeros((D, D), F32)
        for m in range(buffers):
            span = slice(m * rows, (m + 1) * rows)
            ones, count = window_of(sc[span, :], sr[m : m + 1, :])
            trend = (mm(ones, xv[span, :]) / count).astype(BF16)
            target = gv[span, :]
            tpv[span, :] = mm(trend, wv[...]) + bias[6:7, :]
            total += mm_tn(trend, target)
            back = (mm_nt(target, wv[...]) / count).astype(BF16)
            igv[span, :] = mm(ones, back).astype(BF16)
        dwv[...] = total
        all_wait([go.go(tpv, tp), go.go(igv, ig), go.go(dwv, dw)])


def iso_body(sid, down, mask_a, mask_b, bias, gain, w, iso, squash, pad, wbuf, sem):
    def tile_copy(k):
        return pltpu.make_async_copy(w.at[k], wbuf.at[k], sem.at[k])

    @pl.when(sid[0] == 1)
    def _():
        for k in range(DOWN_TILES):
            tile_copy(k).start()
        at = 0
        for member, mask in enumerate((mask_a, mask_b)):
            spots = mask.shape[0]
            own = down[at : at + spots, :].astype(F32)
            pad[0:16, :] = jnp.zeros((16, D), F32)
            pad[16 : 16 + spots, :] = own
            total = jnp.zeros((spots, D), F32)
            for j in range(TAPS[member]):
                tile = FIRST_TAP[member] + j
                moved = (pad[16 - j : 16 - j + spots, :] * mask[:, j : j + 1]).astype(BF16)
                tile_copy(tile).wait()
                total += mm(moved, wbuf[tile])
            flat = jnp.tanh(total + bias[member : member + 1, :])
            squash[at : at + spots, :] = flat
            n, _ = normal(flat + own)
            out = n * gain[member : member + 1, :] + bias[2 + member : 3 + member, :]
            iso[at : at + spots, :] = out.astype(BF16)
            at += spots


def merge_body(sid, iso, season, bias, gain, w, mixed, u, up, ucb, sv, mv, uv, wbuf, sem):
    total_rows = sv.shape[0]
    step = 128

    def tile_copy(k):
        return pltpu.make_async_copy(w.at[k], wbuf.at[k], sem.at[k])

    @pl.when(sid[0] == 2)
    def _():
        for k in range(DOWN_TILES + 2):
            tile_copy(k).start()
        load = pltpu.make_async_copy(season, sv, sem.at[DOWN_TILES + 2])
        load.start()
        at = 0
        for member in range(2):
            stride = STRIDES[member]
            spots = total_rows // stride
            own = iso[at : at + spots, :]
            for k in range(stride):
                tile = FIRST_TILE[member] + k
                tile_copy(tile).wait()
                flat = jnp.tanh(mm(own, wbuf[tile]) + bias[member : member + 1, :])
                spread_set(ucb, (member,), k, spots, stride, flat)
            at += spots
        load.wait()
        tile_copy(DOWN_TILES).wait()
        tile_copy(DOWN_TILES + 1).wait()
        keep = pltpu.make_async_copy(ucb, u, sem.at[DOWN_TILES + 3])
        keep.start()
        for start in range(0, total_rows, step):
            span = slice(start, start + step)
            low = sv[span, :].astype(F32)
            total = jnp.zeros((step, D), F32) + bias[4:5, :]
            for member in range(2):
                n, _ = normal(block_get(ucb, (member,), start, step) + low)
                upward = n * gain[member : member + 1, :] + bias[2 + member : 3 + member, :]
                upward = upward.astype(BF16)
                uv[member, span, :] = upward
                total += mm(upward, wbuf[DOWN_TILES + member])
            mv[span, :] = total.astype(BF16)
        out = pltpu.make_async_copy(mv, mixed, sem.at[DOWN_TILES + 4])
        out.start()
        out_up = pltpu.make_async_copy(uv, up, sem.at[DOWN_TILES + 5])
        out_up.start()
        keep.wait()
        out.wait()
        out_up.wait()


def ffn_body(sid, mixed, cot, tp, bias, gain, w, out, gm, act, gb, dh, small,
             mv, cv, tv, wbuf, ov, gmv, av, gbv, dhv, gd, sem):
    rows = mv.shape[0]
    half = math.sqrt(0.5)
    dense = 1.0 / math.sqrt(2.0 * math.pi)

    @pl.when(sid[0] == 3)
    def _():
        go = Copies(sem)
        loads = [go.go(mixed, mv), go.go(w.at[pl.ds(0, 2 * HIDDEN_TILES)], wbuf)]
        loads += [go.go(cot, cv), go.go(tp, tv)]
        all_wait(loads)
        low = mv[...]
        branch = jnp.zeros((rows, D), F32) + bias[4:5, :]
        for k in range(HIDDEN_TILES):
            h = mm(low, wbuf[k]) + bias[k : k + 1, :]
            share = 0.5 * (1.0 + lax.erf(h * half))
            a = (h * share).astype(BF16)
            gd[k] = share + h * jnp.exp(h * h * -0.5) * dense
            av[k] = a
            branch += mm(a, wbuf[HIDDEN_TILES + k])
        n, scale = normal(low.astype(F32) + branch)
        ov[...] = (n * gain[0:1, :] + bias[5:6, :] + tv[...]).astype(BF16)
        target = cv[...].astype(F32)
        grad = normal_back(target, gain[0:1, :], n, scale)
        grad_low = grad.astype(BF16)
        gbv[...] = grad_low
        shift = col_sum(target)
        small[...] = jnp.zeros((SMALL_ROWS, D), F32)
        small[4:5, :] = col_sum(grad_low.astype(F32))
        small[5:6, :] = shift
        small[6:7, :] = shift
        small[8:9, :] = col_sum(target * n)
        for k in range(HIDDEN_TILES):
            low_k = (mm_nt(grad_low, wbuf[HIDDEN_TILES + k]) * gd[k]).astype(BF16)
            dhv[k] = low_k
            small[k : k + 1, :] = col_sum(low_k.astype(F32))
            grad += mm_nt(low_k, wbuf[k])
        gmv[...] = grad.astype(BF16)
        all_wait(
            [go.go(ov, out), go.go(gmv, gm), go.go(av, act), go.go(gbv, gb), go.go(dhv, dh)]
        )


def ffn_grad_body(count, sid, *refs):
    mixed, act, gb, dh = (refs[i * count : (i + 1) * count] for i in range(4))
    dw8, total, mv, av, gv, dv, tv, wv, sem = refs[4 * count :]

    @pl.when(sid[0] == 3)
    def _():
        go = Copies(sem)
        loads = [go.go(dw8, wv)]
        for c in range(count):
            loads += [go.go(mixed[c], mv.at[c]), go.go(act[c], av.at[c])]
            loads += [go.go(gb[c], gv.at[c]), go.go(dh[c], dv.at[c])]
        all_wait(loads)
        for k in range(HIDDEN_TILES):
            first = jnp.zeros((D, D), F32)
            second = jnp.zeros((D, D), F32)
            for c in range(count):
                first += mm_tn(mv[c], dv[c, k])
                second += mm_tn(av[c, k], gv[c])
            tv[k] = first.astype(BF16)
            tv[HIDDEN_TILES + k] = second.astype(BF16)
        tv[2 * HIDDEN_TILES] = wv[...].astype(BF16)
        go.go(tv, total).wait()


def up_grad_body(first_row, sid, gm, u, season, bias, gain, w, g, gw, small,
                 gmv, uv, sv, wv, gv, gwv, sem):
    rows = gmv.shape[0]
    step = 128

    @pl.when(sid[0] == 2)
    def _():
        go = Copies(sem)
        span = pl.ds(first_row, rows)
        all_wait(
            [
                go.go(gm, gmv),
                go.go(u.at[:, :, span, :], uv),
                go.go(season.at[span, :], sv),
                go.go(w.at[pl.ds(DOWN_TILES, 2)], wv),
            ]
        )
        small[...] = jnp.zeros((SMALL_ROWS, D), F32)
        for start in range(0, rows, step):
            part = slice(start, start + step)
            low = sv[part, :].astype(F32)
            grad_mixed = gmv[part, :]
            small[4:5, :] += col_sum(grad_mixed.astype(F32))
            wire = jnp.zeros((step, D), F32)
            for member in range(2):
                o = mm_nt(grad_mixed, wv[member])
                flat = block_get(uv, (member,), start, step)
                n, scale = normal(flat + low)
                back = normal_back(o, gain[member : member + 1, :], n, scale)
                wire += back
                cell = (back * (1.0 - flat * flat)).astype(BF16).astype(F32)
                block_set(gv, (member,), start, step, cell)
                small[member : member + 1, :] += col_sum(cell)
                small[2 + member : 3 + member, :] += col_sum(o)
                small[8 + member : 9 + member, :] += col_sum(o * n)
            gwv[part, :] = wire
        all_wait([go.go(gv, g), go.go(gwv, gw)])


def up_dx_body(count, sid, *refs):
    g = refs[:count]
    w, out, gv, wbuf, sem = refs[count:]
    total_rows = gv.shape[2]
    rows = total_rows // count

    def tile_copy(k):
        return pltpu.make_async_copy(w.at[k], wbuf.at[k], sem.at[k])

    @pl.when(sid[0] == 2)
    def _():
        loads = [
            pltpu.make_async_copy(
                g[c], gv.at[:, :, pl.ds(c * rows, rows), :], sem.at[DOWN_TILES + c]
            )
            for c in range(count)
        ]
        for load in loads:
            load.start()
        for k in range(DOWN_TILES):
            tile_copy(k).start()
        all_wait(loads)
        at = 0
        for member in range(2):
            stride = STRIDES[member]
            spots = total_rows // stride
            total = jnp.zeros((spots, D), F32)
            for k in range(stride):
                tile = FIRST_TILE[member] + k
                tile_copy(tile).wait()
                cell = spread_get(gv, (member,), k, spots, stride).astype(BF16)
                total += mm_nt(cell, wbuf[tile])
            out[at : at + spots, :] = total.astype(BF16)
            at += spots


def merge_grad_body(count, sid, *refs):
    gm = refs[:count]
    gw = refs[count : 2 * count]
    up, sc, sr, held, ig, total, gmv, gwv, upv, igv, tv, sem = refs[2 * count :]
    buffers, rows = sr.shape
    part = buffers * rows // count

    @pl.when(sid[0] == 2)
    def _():
        go = Copies(sem)
        loads = [go.go(up, upv)]
        for c in range(count):
            loads.append(go.go(gm[c], gmv.at[pl.ds(c * part, part), :]))
            loads.append(go.go(gw[c], gwv.at[pl.ds(c * part, part), :]))
        all_wait(loads)
        for member in range(2):
            tv[member] = mm_tn(upv[member], gmv[...]).astype(BF16)
        for m in range(buffers):
            span = slice(m * rows, (m + 1) * rows)
            ones, count_rows = window_of(sc[span, :], sr[m : m + 1, :])
            wire = gwv[span, :]
            away = mm(ones, (wire / count_rows).astype(BF16))
            igv[span, :] = (wire - away).astype(BF16)
        all_wait([go.go(tv, total.at[pl.ds(0, 2)]), go.go(igv, ig)])


def iso_grad_body(sid, grad, down, squash, back_a, back_b, bias, gain, w, gq, gdown, small,
                  pad, wbuf, sem):
    def tile_copy(k):
        return pltpu.make_async_copy(w.at[k], wbuf.at[k], sem.at[k])

    @pl.when(sid[0] == 1)
    def _():
        for k in range(DOWN_TILES):
            tile_copy(k).start()
        small[...] = jnp.zeros((SMALL_ROWS, D), F32)
        at = 0
        for member, mask in enumerate((back_a, back_b)):
            spots = mask.shape[0]
            span = slice(at, at + spots)
            flat = squash[span, :]
            n, scale = normal(flat + down[span, :].astype(F32))
            o = grad[span, :].astype(F32)
            total = normal_back(o, gain[member : member + 1, :], n, scale)
            cell = (total * (1.0 - flat * flat)).astype(BF16)
            gq[span, :] = cell
            wide = cell.astype(F32)
            small[member : member + 1, :] = col_sum(wide)
            small[2 + member : 3 + member, :] = col_sum(o)
            small[8 + member : 9 + member, :] = col_sum(o * n)
            pad[0:spots, :] = wide
            pad[spots : spots + 16, :] = jnp.zeros((16, D), F32)
            for j in range(TAPS[member]):
                tile = FIRST_TAP[member] + j
                moved = (pad[j : j + spots, :] * mask[:, j : j + 1]).astype(BF16)
                tile_copy(tile).wait()
                total += mm_nt(moved, wbuf[tile])
            gdown[span, :] = total.astype(BF16)
            at += spots


def payload_body(sid, gdown, squash, gq, small_1, small_2, small_3, out):
    spots = gdown.shape[0]

    def put_small(value):
        high = value.astype(BF16)
        out[spots : spots + SMALL_ROWS, :] = high
        out[spots + SMALL_ROWS : spots + 2 * SMALL_ROWS, :] = (value - high.astype(F32)).astype(
            BF16
        )

    @pl.when(sid[0] == 0)
    def _():
        flat = squash[...]
        cell = (gdown[...].astype(F32) * (1.0 - flat * flat)).astype(BF16)
        out[0:spots, :] = cell
        wide = cell.astype(F32)
        cut = (spots // 7) * 4
        rows = lax.broadcasted_iota(jnp.int32, (SMALL_ROWS, D), 0)
        value = jnp.where(rows == 0, col_sum(wide[:cut, :]), 0.0)
        value = jnp.where(rows == 1, col_sum(wide[cut:, :]), value)
        put_small(value)

    @pl.when(sid[0] == 1)
    def _():
        out[0:spots, :] = gq[...]
        put_small(small_1[...])

    @pl.when(sid[0] == 2)
    def _():
        out[0:spots, :] = jnp.zeros((spots, D), BF16)
        put_small(small_2[...])

    @pl.when(sid[0] == 3)
    def _():
        out[0:spots, :] = jnp.zeros((spots, D), BF16)
        put_small(small_3[...])


def feed_grad_body(sid, gp, ig_2, ig_3, sc, sr, w, ig, cb, igv, wbuf, sem):
    buffers, rows = sr.shape
    total_rows = buffers * rows

    def tile_copy(k):
        return pltpu.make_async_copy(w.at[k], wbuf.at[k], sem.at[k])

    @pl.when(sid[0] == 0)
    def _():
        for k in range(DOWN_TILES):
            tile_copy(k).start()
        at = 0
        for member in range(2):
            stride = STRIDES[member]
            spots = total_rows // stride
            cell = gp[at : at + spots, :]
            for k in range(stride):
                tile = FIRST_TILE[member] + k
                tile_copy(tile).wait()
                back = mm_nt(cell, wbuf[tile])
                if member == 1:
                    back += spread_get(cb, (), k, spots, stride)
                spread_set(cb, (), k, spots, stride, back)
            at += spots
        for m in range(buffers):
            span = slice(m * rows, (m + 1) * rows)
            ones, count = window_of(sc[span, :], sr[m : m + 1, :])
            season = block_get(cb, (), m * rows, rows)
            igv[span, :] = (season - mm(ones, (season / count).astype(BF16))).astype(BF16)
        copy = pltpu.make_async_copy(igv, ig, sem.at[DOWN_TILES])
        copy.start()
        copy.wait()

    @pl.when(sid[0] == 1)
    def _():
        igv[...] = jnp.zeros(igv.shape, BF16)
        copy = pltpu.make_async_copy(igv, ig, sem.at[DOWN_TILES])
        copy.start()
        copy.wait()

    @pl.when(sid[0] == 2)
    def _():
        copy = pltpu.make_async_copy(ig_2, ig, sem.at[DOWN_TILES])
        copy.start()
        copy.wait()

    @pl.when(sid[0] == 3)
    def _():
        copy = pltpu.make_async_copy(ig_3, ig, sem.at[DOWN_TILES])
        copy.start()
        copy.wait()


def season_flip_body(sid, season, out_a, out_b, sv, cb, st_a, st_b, sem):
    rows = sv.shape[0]
    groups = season.shape[0] // rows

    @pl.when(sid[0] == 0)
    def _():
        def group(i, carry):
            load = pltpu.make_async_copy(season.at[pl.ds(i * rows, rows), :], sv, sem.at[0])
            load.start()
            load.wait()

            def widen(r, inner):
                at = pl.multiple_of(r * 256, 256)
                block_set(cb, (), at, 256, sv[pl.ds(at, 256), :].astype(F32))
                return inner

            lax.fori_loop(0, rows // 256, widen, 0)
            for member, stage in enumerate((st_a, st_b)):
                stride = STRIDES[member]
                spots = rows // stride

                def flip(k, inner, stage=stage, stride=stride, spots=spots):
                    stage[k] = spread_get(cb, (), k, spots, stride).T.astype(BF16)
                    return inner

                lax.fori_loop(0, stride, flip, 0)
            spots_a, spots_b = rows // SCALE_A, rows // SCALE_B
            copies = [
                pltpu.make_async_copy(
                    st_a, out_a.at[:, :, pl.ds(pl.multiple_of(i * spots_a, 128), spots_a)], sem.at[1]
                ),
                pltpu.make_async_copy(
                    st_b, out_b.at[:, :, pl.ds(pl.multiple_of(i * spots_b, 128), spots_b)], sem.at[2]
                ),
            ]
            for copy in copies:
                copy.start()
            all_wait(copies)
            return carry

        lax.fori_loop(0, groups, group, 0)


def up_grad_all_body(sid, gm, season, iso, bias, gain, w, out_a, out_b,
                     gmv, sv, isov, cb, ocb, st_a, st_b, wbuf, sem):
    rows = gmv.shape[0]
    blocks = gm.shape[0]
    step = 256

    @pl.when(sid[0] == 2)
    def _():
        load = pltpu.make_async_copy(w, wbuf, sem.at[0])
        load.start()
        load.wait()

        def block(i, carry):
            go = Copies(sem)
            all_wait(
                [
                    go.go(gm.at[i], gmv),
                    go.go(season.at[pl.ds(pl.multiple_of(i * rows, 128), rows), :], sv),
                    go.go(iso.at[i], isov),
                ]
            )

            def widen(r, inner):
                at = pl.multiple_of(r * step, step)
                block_set(cb, (), at, step, sv[pl.ds(at, step), :].astype(F32))
                for member in range(2):
                    o = mm_nt(gmv[pl.ds(at, step), :], wbuf[DOWN_TILES + member])
                    block_set(ocb, (member,), at, step, o)
                return inner

            lax.fori_loop(0, rows // step, widen, 0)
            at = 0
            for member, stage in enumerate((st_a, st_b)):
                stride = STRIDES[member]
                spots = rows // stride

                def tile(k, inner, stage=stage, stride=stride, spots=spots, at=at, member=member):
                    own = isov[at : at + spots, :]
                    flat = mm(own, wbuf[FIRST_TILE[member] + k]) + bias[member : member + 1, :]
                    flat = jnp.tanh(flat)
                    n, scale = normal(flat + spread_get(cb, (), k, spots, stride))
                    o = spread_get(ocb, (member,), k, spots, stride)
                    back = normal_back(o, gain[member : member + 1, :], n, scale)
                    stage[k] = (back * (1.0 - flat * flat)).astype(BF16)
                    return inner

                lax.fori_loop(0, stride, tile, 0)
                at += spots
            spots_a, spots_b = rows // SCALE_A, rows // SCALE_B
            all_wait(
                [
                    go.go(st_a, out_a.at[:, pl.ds(pl.multiple_of(i * spots_a, 32), spots_a), :]),
                    go.go(st_b, out_b.at[:, pl.ds(pl.multiple_of(i * spots_b, 32), spots_b), :]),
                ]
            )
            return carry

        lax.fori_loop(0, blocks, block, 0)


def tile_grad_body(sid, pay_1, pay_2, flip_a, flip_b, cell_a, cell_b, art, back_a, back_b,
                   tiles, bias_out, gain_out,
                   flat, turned, left, right, stage, sv, sem):
    blocks = pay_1.shape[0]
    spots_of = (back_a.shape[0] // blocks, back_b.shape[0] // blocks)
    first_spot = (0, spots_of[0])
    spots_all = spots_of[0] + spots_of[1]
    per = 8
    groups = blocks // per
    lead = sid[0]

    def out_copy(tile, slot):
        return pltpu.make_async_copy(stage.at[slot], tiles.at[tile], sem.at[slot])

    all_small = [
        pltpu.make_async_copy(pay_2.at[i, pl.ds(spots_all, 2 * SMALL_ROWS), :], sv.at[i], sem.at[8])
        for i in range(blocks)
    ]
    for copy in all_small:
        copy.start()
        copy.wait()
    summed = jnp.zeros((SMALL_ROWS, D), F32)
    for i in range(blocks):
        summed += sv[i, 0:SMALL_ROWS, :].astype(F32) + sv[i, SMALL_ROWS:, :].astype(F32)
    bias_out[...] = summed[0:7, :]
    gain_out[...] = summed[8:10, :]

    def run(member, count, first_out, source, operand):
        spots = per * spots_of[member]
        steps = count * groups

        def fetch(t, slot):
            k, g = t // groups, t % groups
            at = pl.multiple_of(g * spots, 256)
            if source == "left":
                ref = (flip_a, flip_b)[member]
                return pltpu.make_async_copy(
                    ref.at[k, :, pl.ds(at, spots)], left.at[slot, :, pl.ds(0, spots)], sem.at[4 + slot]
                )
            ref = (cell_a, cell_b)[member]
            return pltpu.make_async_copy(
                ref.at[k, pl.ds(at, spots), :], right.at[slot, pl.ds(0, spots), :], sem.at[4 + slot]
            )

        if source:
            fetch(0, 0).start()

        def step(t, carry):
            slot = t % 2
            k, g = t // groups, t % groups
            if source:

                @pl.when(t + 1 < steps)
                def _():
                    fetch(t + 1, 1 - slot).start()

                fetch(t, slot).wait()
            out_slot = k % 2

            @pl.when(jnp.logical_and(g == 0, k >= 2))
            def _():
                out_copy(first_out + k - 2, out_slot).wait()

            value = operand(k, g, slot, spots)

            @pl.when(g == 0)
            def _():
                stage[out_slot] = value

            @pl.when(g > 0)
            def _():
                stage[out_slot] += value

            @pl.when(g == groups - 1)
            def _():
                out_copy(first_out + k, out_slot).start()

            return carry

        lax.fori_loop(0, steps, step, 0)
        out_copy(first_out + count - 2, (count - 2) % 2).wait()
        out_copy(first_out + count - 1, (count - 1) % 2).wait()

    def take(pay, member):
        spots = spots_of[member]
        copies = [
            pltpu.make_async_copy(
                pay.at[i, pl.ds(first_spot[member], spots), :],
                flat.at[pl.ds(i * spots, spots), :],
                sem.at[8],
            )
            for i in range(blocks)
        ]
        for copy in copies:
            copy.start()
            copy.wait()

    def turn(member):
        spots = per * spots_of[member]

        def one(g, carry):
            at = pl.multiple_of(g * spots, 256)
            turned[:, pl.ds(at, spots)] = flat[pl.ds(at, spots), :].astype(F32).T.astype(BF16)
            return carry

        lax.fori_loop(0, groups, one, 0)

    def blank(first, last):
        stage[0] = jnp.zeros((D, D), F32)
        for tile in range(first, last):
            out_copy(tile, 0).start()
            out_copy(tile, 0).wait()

    @pl.when(lead == 0)
    def _():
        for member in range(2):
            take(pay_2, member)

            def operand(k, g, slot, spots):
                at = pl.multiple_of(g * spots, 256)
                return mm(left[slot, :, 0:spots], flat[pl.ds(at, spots), :])

            run(member, STRIDES[member], FIRST_TILE[member], "left", operand)
        blank(DOWN_TILES, tiles.shape[0])

    @pl.when(lead == 1)
    def _():
        for member in range(2):
            take(pay_1, member)
            turn(member)
            take(pay_2, member)
            mask = (back_a, back_b)[member]

            def operand(k, g, slot, spots, mask=mask):
                at = pl.multiple_of(g * spots, 256)
                wide = jnp.concatenate(
                    [flat[pl.ds(at, spots), :].astype(F32)], 0
                )
                moved = pltpu.roll(wide, lax.rem(spots - k, spots), 0)
                lane = lax.broadcasted_iota(jnp.int32, (spots, mask.shape[1]), 1)
                hit = jnp.sum(
                    jnp.where(lane == k, mask[pl.ds(at, spots), :], 0.0), axis=1, keepdims=True
                )
                return mm(turned[:, pl.ds(at, spots)], (moved * hit).astype(BF16))

            run(member, TAPS[member], FIRST_TAP[member], "", operand)
        blank(DOWN_TILES, tiles.shape[0])

    @pl.when(lead == 2)
    def _():
        for member in range(2):
            take(pay_1, member)
            turn(member)

            def operand(k, g, slot, spots):
                at = pl.multiple_of(g * spots, 256)
                return mm(turned[:, pl.ds(at, spots)], right[slot, 0:spots, :])

            run(member, STRIDES[member], FIRST_TILE[member], "right", operand)
        for member in range(2):
            load = pltpu.make_async_copy(art.at[member], right.at[0, pl.ds(0, D), :], sem.at[8])
            load.start()
            load.wait()
            stage[0] = right[0, 0:D, :].astype(F32)
            out_copy(DOWN_TILES + member, 0).start()
            out_copy(DOWN_TILES + member, 0).wait()

    @pl.when(lead == 3)
    def _():
        for k in range(2 * HIDDEN_TILES + 1):
            load = pltpu.make_async_copy(art.at[k], right.at[0, pl.ds(0, D), :], sem.at[8])
            load.start()
            load.wait()
            stage[0] = right[0, 0:D, :].astype(F32)
            out_copy(k, 0).start()
            out_copy(k, 0).wait()
        blank(2 * HIDDEN_TILES + 1, tiles.shape[0])


def shifted_masks(spot_series, taps, forward):
    buffers, spots = spot_series.shape
    fill = jnp.full((buffers, taps), -1, spot_series.dtype)
    if forward:
        padded = jnp.concatenate([fill, spot_series], 1)
        moved = [padded[:, taps - j : taps - j + spots] for j in range(taps)]
    else:
        padded = jnp.concatenate([spot_series, fill], 1)
        moved = [padded[:, j : j + spots] for j in range(taps)]
    hits = [(part == spot_series).astype(F32) for part in moved]
    return jnp.stack(hits, 2).reshape(buffers * spots, taps)


def shards(inputs, weights, biases, gain_rows, block_series, cotangent):
    section = lax.axis_index("section")
    sections = lax.axis_size("section")
    dp = lax.axis_size("dp")
    buffers = block_series.shape[0]
    total_rows = inputs.shape[0]
    rows = total_rows // buffers
    tile_count = weights.shape[0]
    spots_a, spots_b = total_rows // SCALE_A, total_rows // SCALE_B
    spots = spots_a + spots_b
    sid = section.astype(jnp.int32).reshape(1)
    row_series = jnp.repeat(block_series, BLOCK, axis=1)
    sc = row_series.reshape(total_rows, 1)
    sr = row_series
    spot_series_a = jnp.repeat(block_series, BLOCK // SCALE_A, axis=1)
    spot_series_b = jnp.repeat(block_series, BLOCK // SCALE_B, axis=1)
    tile = (D, D)

    def permute(value, source, target):
        return lax.ppermute(value, "section", [(source, target)])

    season, down, squash_0 = call(
        season_body,
        "season",
        [(sid, "s"), (inputs, "v"), (sc, "v"), (sr, "v"), (biases, "v"), (weights, "a")],
        [((total_rows, D), BF16, "v"), ((spots, D), BF16, "v"), ((spots, D), F32, "v")],
        [
            pltpu.VMEM((COLS, total_rows, LANES), F32),
            pltpu.VMEM((DOWN_TILES,) + tile, BF16),
            sems(DOWN_TILES),
        ],
        flops=4 * 10**9,
        moved=20 * 10**6,
    )
    down_in = permute(down, 0, 1)
    season_all = lax.all_gather(season, "dp", axis=0, tiled=True)
    tp, ig_3, dw8 = call(
        trend_body,
        "trend",
        [(sid, "s"), (inputs, "a"), (cotangent, "a"), (sc, "v"), (sr, "v"), (biases, "v"),
         (weights, "a")],
        [((total_rows, D), F32, "a"), ((total_rows, D), BF16, "a"), (tile, F32, "a")],
        [
            pltpu.VMEM((total_rows, D), BF16),
            pltpu.VMEM((total_rows, D), BF16),
            pltpu.VMEM((total_rows, D), F32),
            pltpu.VMEM((total_rows, D), BF16),
            pltpu.VMEM(tile, F32),
            pltpu.VMEM(tile, BF16),
            sems(6),
        ],
        flops=5 * 10**9,
        moved=10 * 10**6,
    )
    iso, squash_1 = call(
        iso_body,
        "iso",
        [(sid, "s"), (down_in, "v"), (shifted_masks(spot_series_a, TAPS_A, True), "v"),
         (shifted_masks(spot_series_b, TAPS_B, True), "v"), (biases, "v"), (gain_rows, "v"),
         (weights, "a")],
        [((spots, D), BF16, "v"), ((spots, D), F32, "v")],
        [
            pltpu.VMEM((16 + spots_a, D), F32),
            pltpu.VMEM((DOWN_TILES,) + tile, BF16),
            sems(DOWN_TILES),
        ],
        flops=2 * 10**9,
        moved=15 * 10**6,
    )
    iso_in = permute(iso, 1, 2)
    spread = jnp.where(section == 1, down_in, iso_in)
    numbers = jnp.zeros((SMALL_ROWS, D), BF16)
    numbers = numbers.at[0, :spots_a].set(spot_series_a.reshape(-1).astype(BF16))
    numbers = numbers.at[1, :spots_b].set(spot_series_b.reshape(-1).astype(BF16))
    pay_1 = lax.all_gather(jnp.concatenate([spread, numbers], 0), "dp", axis=0, tiled=False)
    mixed, u, up = call(
        merge_body,
        "merge",
        [(sid, "s"), (iso_in, "v"), (season, "a"), (biases, "v"), (gain_rows, "v"), (weights, "a")],
        [((total_rows, D), BF16, "a"), ((2, COLS, total_rows, LANES), F32, "a"),
         ((2, total_rows, D), BF16, "a")],
        [
            pltpu.VMEM((2, COLS, total_rows, LANES), F32),
            pltpu.VMEM((total_rows, D), BF16),
            pltpu.VMEM((total_rows, D), BF16),
            pltpu.VMEM((2, total_rows, D), BF16),
            pltpu.VMEM((DOWN_TILES + 2,) + tile, BF16),
            sems(DOWN_TILES + 6),
        ],
        flops=4 * 10**9,
        moved=25 * 10**6,
    )

    def ffn(mixed_part, first):
        part = mixed_part.shape[0]
        span = slice(first, first + part)
        return call(
            ffn_body,
            "ffn",
            [(sid, "s"), (mixed_part, "a"), (cotangent[span], "a"), (tp[span], "a"), (biases, "v"),
             (gain_rows, "v"), (weights, "a")],
            [((part, D), BF16, "a"), ((part, D), BF16, "a"), ((HIDDEN_TILES, part, D), BF16, "a"),
             ((part, D), BF16, "a"), ((HIDDEN_TILES, part, D), BF16, "a"),
             ((SMALL_ROWS, D), F32, "v")],
            [
                pltpu.VMEM((part, D), BF16),
                pltpu.VMEM((part, D), BF16),
                pltpu.VMEM((part, D), F32),
                pltpu.VMEM((2 * HIDDEN_TILES,) + tile, BF16),
                pltpu.VMEM((part, D), BF16),
                pltpu.VMEM((part, D), BF16),
                pltpu.VMEM((HIDDEN_TILES, part, D), BF16),
                pltpu.VMEM((part, D), BF16),
                pltpu.VMEM((HIDDEN_TILES, part, D), BF16),
                pltpu.VMEM((HIDDEN_TILES, part, D), F32),
                sems(10),
            ],
            flops=6 * part * D * 4 * D * 2,
            moved=20 * 10**6,
        )

    count = buffers
    mixed_in, results = [], []
    for c in range(count):
        part = permute(mixed[c * rows : (c + 1) * rows], 2, 3)
        mixed_in.append(part)
        results.append(ffn(part, c * rows))
    small_3 = sum(r[5] for r in results)
    gm_in = [permute(r[1], 3, 2) for r in results]
    art = call(
        lambda *refs: ffn_grad_body(count, *refs),
        "ffn_grad",
        [(sid, "s")]
        + [(part, "a") for part in mixed_in]
        + [(r[2], "a") for r in results]
        + [(r[3], "a") for r in results]
        + [(r[4], "a") for r in results]
        + [(dw8, "a")],
        [((2 * HIDDEN_TILES + 1,) + tile, BF16, "a")],
        [
            pltpu.VMEM((count, rows, D), BF16),
            pltpu.VMEM((count, HIDDEN_TILES, rows, D), BF16),
            pltpu.VMEM((count, rows, D), BF16),
            pltpu.VMEM((count, HIDDEN_TILES, rows, D), BF16),
            pltpu.VMEM((2 * HIDDEN_TILES + 1,) + tile, BF16),
            pltpu.VMEM(tile, F32),
            sems(4 * count + 2),
        ],
        flops=16 * total_rows * D * D,
        moved=25 * 10**6,
    )[0]
    ups = []
    for c in range(count):
        ups.append(
            call(
                lambda *refs, c=c: up_grad_body(c * rows, *refs),
                "up_grad",
                [(sid, "s"), (gm_in[c], "a"), (u, "a"), (season, "a"), (biases, "v"),
                 (gain_rows, "v"), (weights, "a")],
                [((2, COLS, rows, LANES), F32, "a"), ((rows, D), F32, "a"),
                 ((SMALL_ROWS, D), F32, "v")],
                [
                    pltpu.VMEM((rows, D), BF16),
                    pltpu.VMEM((2, COLS, rows, LANES), F32),
                    pltpu.VMEM((rows, D), BF16),
                    pltpu.VMEM((2,) + tile, BF16),
                    pltpu.VMEM((2, COLS, rows, LANES), F32),
                    pltpu.VMEM((rows, D), F32),
                    sems(6),
                ],
                flops=2 * 10**9,
                moved=6 * 10**6,
            )
        )
    small_2 = sum(r[2] for r in ups)
    giso = call(
        lambda *refs: up_dx_body(count, *refs),
        "up_dx",
        [(sid, "s")] + [(r[0], "a") for r in ups] + [(weights, "a")],
        [((spots, D), BF16, "v")],
        [
            pltpu.VMEM((2, COLS, total_rows, LANES), F32),
            pltpu.VMEM((DOWN_TILES,) + tile, BF16),
            sems(DOWN_TILES + count),
        ],
        flops=2 * 10**9,
        moved=20 * 10**6,
    )[0]
    giso_in = permute(giso, 2, 1)
    gm_all = lax.all_gather(jnp.concatenate(gm_in, 0), "dp", axis=0, tiled=False)
    ig_2, art = call(
        lambda *refs: merge_grad_body(count, *refs),
        "merge_grad",
        [(sid, "s")]
        + [(part, "a") for part in gm_in]
        + [(r[1], "a") for r in ups]
        + [(up, "a"), (sc, "v"), (sr, "v"), (art, "a")],
        [((total_rows, D), BF16, "a"), (art.shape, BF16, "a")],
        [
            pltpu.VMEM((total_rows, D), BF16),
            pltpu.VMEM((total_rows, D), F32),
            pltpu.VMEM((2, total_rows, D), BF16),
            pltpu.VMEM((total_rows, D), BF16),
            pltpu.VMEM((2,) + tile, BF16),
            sems(2 * count + 3),
        ],
        flops=4 * 10**9,
        moved=15 * 10**6,
        aliases={2 * count + 4: 1},
    )
    art = lax.psum(art, "dp")
    gq, gdown, small_1 = call(
        iso_grad_body,
        "iso_grad",
        [(sid, "s"), (giso_in, "v"), (down_in, "v"), (squash_1, "v"),
         (shifted_masks(spot_series_a, TAPS_A, False), "v"),
         (shifted_masks(spot_series_b, TAPS_B, False), "v"),
         (biases, "v"), (gain_rows, "v"), (weights, "a")],
        [((spots, D), BF16, "v"), ((spots, D), BF16, "v"), ((SMALL_ROWS, D), F32, "v")],
        [
            pltpu.VMEM((16 + spots_a, D), F32),
            pltpu.VMEM((DOWN_TILES,) + tile, BF16),
            sems(DOWN_TILES),
        ],
        flops=2 * 10**9,
        moved=15 * 10**6,
    )
    gdown_in = permute(gdown, 1, 0)
    payload = call(
        payload_body,
        "payload",
        [(sid, "s"), (gdown_in, "v"), (squash_0, "v"), (gq, "v"), (small_1, "v"), (small_2, "v"),
         (small_3, "v")],
        [((spots + 2 * SMALL_ROWS, D), BF16, "v")],
        [],
        moved=10**6,
    )[0]
    pay_2 = lax.all_gather(payload, "dp", axis=0, tiled=False)
    ig = call(
        feed_grad_body,
        "feed_grad",
        [(sid, "s"), (payload, "v"), (ig_2, "a"), (ig_3, "a"), (sc, "v"), (sr, "v"), (weights, "a")],
        [((total_rows, D), BF16, "a")],
        [
            pltpu.VMEM((COLS, total_rows, LANES), F32),
            pltpu.VMEM((total_rows, D), BF16),
            pltpu.VMEM((DOWN_TILES,) + tile, BF16),
            sems(DOWN_TILES + 1),
        ],
        flops=2 * 10**9,
        moved=20 * 10**6,
    )[0]
    ig = lax.psum_scatter(ig, "section", scatter_dimension=1, tiled=True)
    group = 4 * total_rows
    flip_a, flip_b = call(
        season_flip_body,
        "season_flip",
        [(sid, "s"), (season_all, "a")],
        [((SCALE_A, D, dp * spots_a), BF16, "a"), ((SCALE_B, D, dp * spots_b), BF16, "a")],
        [
            pltpu.VMEM((group, D), BF16),
            pltpu.VMEM((COLS, group, LANES), F32),
            pltpu.VMEM((SCALE_A, D, group // SCALE_A), BF16),
            pltpu.VMEM((SCALE_B, D, group // SCALE_B), BF16),
            sems(3),
        ],
        flops=10**9,
        moved=40 * 10**6,
    )
    cell_a, cell_b = call(
        up_grad_all_body,
        "up_grad_all",
        [(sid, "s"), (gm_all, "a"), (season_all, "a"), (pay_1, "a"), (biases, "v"),
         (gain_rows, "v"), (weights, "a")],
        [((SCALE_A, dp * spots_a, D), BF16, "a"), ((SCALE_B, dp * spots_b, D), BF16, "a")],
        [
            pltpu.VMEM((total_rows, D), BF16),
            pltpu.VMEM((total_rows, D), BF16),
            pltpu.VMEM((spots + SMALL_ROWS, D), BF16),
            pltpu.VMEM((COLS, total_rows, LANES), F32),
            pltpu.VMEM((2, COLS, total_rows, LANES), F32),
            pltpu.VMEM((SCALE_A, spots_a, D), BF16),
            pltpu.VMEM((SCALE_B, spots_b, D), BF16),
            pltpu.VMEM((tile_count,) + tile, BF16),
            sems(6),
        ],
        flops=25 * 10**9,
        moved=60 * 10**6,
    )
    number_a = pay_1[:, spots, :spots_a].astype(jnp.int32).reshape(dp * buffers, rows // SCALE_A)
    number_b = pay_1[:, spots + 1, :spots_b].astype(jnp.int32).reshape(dp * buffers, rows // SCALE_B)
    per = 8
    tiles, bias_grad, gain_grad = call(
        tile_grad_body,
        "tile_grad",
        [(sid, "s"), (pay_1, "a"), (pay_2, "a"), (flip_a, "a"), (flip_b, "a"), (cell_a, "a"),
         (cell_b, "a"), (art, "a"), (shifted_masks(number_a, TAPS_A, False), "v"),
         (shifted_masks(number_b, TAPS_B, False), "v")],
        [((tile_count,) + tile, F32, "a"), ((7, D), F32, "v"), ((2, D), F32, "v")],
        [
            pltpu.VMEM((dp * spots_a, D), BF16),
            pltpu.VMEM((D, dp * spots_a), BF16),
            pltpu.VMEM((2, D, per * spots_a), BF16),
            pltpu.VMEM((2, per * spots_a, D), BF16),
            pltpu.VMEM((2,) + tile, F32),
            pltpu.VMEM((dp, 2 * SMALL_ROWS, D), BF16),
            sems(9),
        ],
        flops=13 * 10**9,
        moved=60 * 10**6,
    )
    width = D // sections
    layer = jnp.concatenate([r[0] for r in results], 0)
    shares = [layer[:, j * width : (j + 1) * width] for j in range(sections)]
    own = jnp.where(section == sections - 1, shares[-1], jnp.zeros((), BF16))
    for j in range(sections - 1):
        own += permute(shares[j], sections - 1, j)
    return own, ig.astype(F32), tiles, bias_grad, gain_grad


def solution(mesh):
    return jax.shard_map(
        shards,
        mesh=mesh,
        in_specs=(
            P("dp", None),
            P("section", None, None),
            P("section", None),
            P("section", None),
            P("dp", None),
            P("dp", None),
        ),
        out_specs=(
            P("dp", "section"),
            P("dp", "section"),
            P("section", None, None),
            P("section", None),
            P("section", None),
        ),
        check_vma=False,
    )
```

time: 1770 us -> 725 us (0.41)
  waiting for transfers between devices: 720 us -> 271 us
  Pallas kernels: 0 us -> 365 us
  local copies, waits for them, and re-layouts: 269 us -> 36.3 us
  other arithmetic: 234 us -> 8.29 us
  loops' own time: 208 us -> 0 us
  matrix products: 166 us -> 0 us
  starting transfers between devices: 110 us -> 18 us
  blocking collectives: 28.4 us -> 0 us
    pallas_call x0 -> x21, Pallas kernels: none -> 365 us  [call(): pl.pallas_call(body, name=name, out_shape=[jax.ShapeDtypeStruct(shape, ki...]
    reduce_scatter x1 -> x0, waiting for transfers between devices: 308 us -> none  [shards(): lax.psum_scatter(grad_sums, 'dp', scatter_dimension=1, tiled=True)]
    another operation x14 -> x0, loops' own time: 208 us -> none  [the longest x7 152 us: shards(): lax.switch(branch, backward_list, weights, biases, gain_rows, series, fee...]
    another operation x32 -> x95, local copies, waits for them, and re-layouts: 184 us -> 13 us  [the longest x94 11.8 us: shifted_masks(): return jnp.stack(hits, 2).reshape(buffers * spots, taps)]
    dot_general x56 -> x0, matrix products: 166 us -> none  [the longest x8 41.6 us: backward_third(): lax.dot_general(grad_cells, kernel, (((1, 2), (0, 2)), ((), ())), preferr...]
    ppermute x12 -> x15, waiting for transfers between devices: 176 us -> 68.3 us  [permute(): return lax.ppermute(value, 'section', [(source, target)])]
    ppermute x12 -> x15, starting transfers between devices: 110 us -> 17.8 us  [permute(): return lax.ppermute(value, 'section', [(source, target)])]
    unnamed x10 -> x7, waiting for transfers between devices: 93.2 us -> 6.84 us
  transfers between devices with their start and end apart: 18 -> 21, of which waited for: 18 -> 10; matrix products, arithmetic and copies ran while one was open for 4% -> 4% of each run, Pallas kernels for 0% -> 39%
where the time goes in v1:
time: 725 us; the launch traced here: 715 us
  Pallas kernels  365 us (50%)
  waiting for transfers between devices  271 us (37%)
  local copies, waits for them, and re-layouts  36.3 us (5%)
  starting transfers between devices  18 us (2%)
  between operations  16.3 us (2%)
  other arithmetic  8.29 us (1%)
    pallas_call x21, Pallas kernels, call(): pl.pallas_call(body, name=name, out_shape=[jax.ShapeDtypeStruct(shape, ki...  365 us
    all_gather x1, waiting for transfers between devices, shards(): lax.all_gather(jnp.concatenate(gm_in, 0), 'dp', axis=0, tiled=False)  117 us
    all_gather x1, waiting for transfers between devices, shards(): season_all = lax.all_gather(season, 'dp', axis=0, tiled=True)  79.3 us
    ppermute x15, waiting for transfers between devices, permute(): return lax.ppermute(value, 'section', [(source, target)])  68.3 us
    ppermute x15, starting transfers between devices, permute(): return lax.ppermute(value, 'section', [(source, target)])  17.8 us
  transfers between devices with their start and end apart: 21, of which 10 were waited for; matrix products, arithmetic and copies ran while one was open for 4% of the time, Pallas kernels for 39%

profile of v1, /device:TPU:5, one launch (start us, length us, event | category | flops | bytes accessed | tf_op | source)
XLA Modules:
  0.0 715.0 jit_solution(15549287312826744515)
XLA Ops:
  10.7 4.5 season.1
  21.7 3.6 fusion.83
  25.9 2.4 iso.1
  30.8 12.2 %collective-permute-done.1.iso = bf16[224,512]{1,0:T(8,128)(2,1)S(1)} collective-permute-done((bf16[224,512]{1,0:T(8,128)(2,1)}, bf16[224,512]{1,0:T(8,128)(2,1)S(1)}, u32[]{:S(2)}, u32[]{:S(2)}) %collective-permute-start.1) | collective-permute-done | bytes 229408 | tf_op jit(solution)/shard_map/ppermute | solution.py:878
  43.8 15.7 %merge.1 = (bf16[1536,512]{1,0:T(8,128)(2,1)}, f32[2,4,1536,128]{3,2,1,0:T(8,128)}, bf16[2,1536,512]{2,1,0:T(8,128)(2,1)}) custom-call(s32[1]{0:T(128)} %bitcast.2.sid.refs_0_, bf16[224,512]{1,0:T(8,128)(2,1)} %copy-done.11, bf16[1536,512]{1,0:T(8,128)(2,1)} %get-tuple-element.90.season.refs_3_, f32[7,512]{1,0:T(8,128)} %bias.19, f32[2,512]{1,0:T(2,128)} %gain.15, ...), custom_call_target="tpu_custom_call" | custom-call | flops 4000000000 | bytes 25000000 | tf_op jit(solution)/shard_map/merge/pallas_call | solution.py:98
  59.5 1.5 fusion.86
  72.2 1.9 ffn.4
  75.5 19.6 %collective-permute-done.3.mixed.refs_2_ = bf16[384,512]{1,0:T(8,128)(2,1)S(1)} collective-permute-done((bf16[384,512]{1,0:T(8,128)(2,1)S(1)}, bf16[384,512]{1,0:T(8,128)(2,1)S(1)}, u32[]{:S(2)}, u32[]{:S(2)}) %collective-permute-start.3) | collective-permute-done | bytes 393248 | tf_op jit(solution)/shard_map/ppermute | solution.py:878
  95.9 1.4 ffn.5
  99.4 1.6 ffn.6
  106.5 6.4 up_grad.4
  112.9 5.0 collective-permute-done.10.refs_1_.refs_2_
  118.7 6.5 up_grad.5
  125.2 5.9 collective-permute-done.11.refs_1_.refs_3_
  131.8 6.7 up_grad.6
  138.6 5.5 collective-permute-done.12.refs_1_.refs_4_
  144.8 6.5 up_grad.7
  151.3 9.7 %up_dx.1 = bf16[224,512]{1,0:T(8,128)(2,1)} custom-call(s32[1]{0:T(128)} %bitcast.2.sid.refs_0_, f32[2,4,384,128]{3,2,1,0:T(8,128)} %get-tuple-element.99.refs_1_, f32[2,4,384,128]{3,2,1,0:T(8,128)} %get-tuple-element.101.refs_2_, f32[2,4,384,128]{3,2,1,0:T(8,128)} %get-tuple-element.103.refs_3_, f32[2,4,384,128]{3,2,1,0:T(8,128)} %get-tuple-element.105.refs_4_, ...), custom_call_target="tpu_custom_call" | custom-call | flops 2000000000 | bytes 20000000 | tf_op jit(solution)/shard_map/up_dx/pallas_call | solution.py:98
  163.8 1.8 collective-permute-done.13.grad
  166.3 2.3 iso_grad.1
  169.3 8.3 %merge_grad.1 = (bf16[1536,512]{1,0:T(8,128)(2,1)}, bf16[9,512,512]{2,1,0:T(8,128)(2,1)}) custom-call(s32[1]{0:T(128)} %bitcast.2.sid.refs_0_, bf16[384,512]{1,0:T(8,128)(2,1)} %copy-done.3, bf16[384,512]{1,0:T(8,128)(2,1)} %copy-done.5, bf16[384,512]{1,0:T(8,128)(2,1)} %copy-done.7, bf16[384,512]{1,0:T(8,128)(2,1)} %copy-done.9, ...), custom_call_target="tpu_custom_call", output_to_operand_aliasing={{1}: (12, {})} | custom-call | flops 4000000000 | bytes 15000000 | tf_op jit(solution)/shard_map/merge_grad/pallas_call | solution.py:98
  179.0 2.1 payload.1.gp
  181.1 50.2 %feed_grad.1 = bf16[1536,512]{1,0:T(8,128)(2,1)} custom-call(s32[1]{0:T(128)} %bitcast.2.sid.refs_0_, bf16[256,512]{1,0:T(8,128)(2,1)} %payload.1.gp, bf16[1536,512]{1,0:T(8,128)(2,1)} %get-tuple-element.137.ig_2, bf16[1536,512]{1,0:T(8,128)(2,1)} %get-tuple-element.138.ig_3, s32[1536,1]{1,0:T(8,128)} %reshape_reshape.6.sc.refs_10_, ...), custom_call_target="tpu_custom_call" | custom-call | flops 2000000000 | bytes 20000000 | tf_op jit(solution)/shard_map/feed_grad/pallas_call | solution.py:98
  231.3 2.6 copy.156
  240.6 1.4 collective-permute-start.7
  242.0 18.2 %collective-permute-done.8 = bf16[1536,128]{1,0:T(8,128)(2,1)S(1)} collective-permute-done((bf16[1536,128]{1,0:T(8,128)(2,1)S(1)}, bf16[1536,128]{1,0:T(8,128)(2,1)S(1)}, u32[]{:S(2)}, u32[]{:S(2)}) %collective-permute-start.8) | collective-permute-done | bytes 393248 | tf_op jit(solution)/shard_map/ppermute | solution.py:878
  260.2 1.8 fusion.2
  268.3 5.6 reduce-scatter.4.cloned.1.call-done
  276.0 79.3 %all-gather.8.cloned.1.call-done.season = bf16[12288,512]{1,0:T(8,128)(2,1)} async-done(((bf16[1536,512]{1,0:T(8,128)(2,1)}), bf16[12288,512]{1,0:T(8,128)(2,1)}) %all-gather.8.cloned.1.call-update) | async-done | bytes 12582928 | tf_op jit(solution)/shard_map/all_gather | solution.py:894
  355.4 116.6 %all-gather.14.cloned.1.call-done = bf16[12288,512]{1,0:T(8,128)(2,1)} async-done(((bf16[1536,512]{1,0:T(8,128)(2,1)}), bf16[12288,512]{1,0:T(8,128)(2,1)}) %all-gather.14.cloned.1.call-update) | async-done | bytes 12582928 | tf_op jit(solution)/shard_map/all_gather | solution.py:1048
  472.0 175.1 %up_grad_all.1 = (bf16[12,1024,512]{2,1,0:T(8,128)(2,1)}, bf16[16,768,512]{2,1,0:T(8,128)(2,1)}) custom-call(s32[1]{0:T(128)} %bitcast.2.sid.refs_0_, bf16[8,1536,512]{2,1,0:T(8,128)(2,1)} %bitcast.13, bf16[12288,512]{1,0:T(8,128)(2,1)} %all-gather.8.cloned.1.call-done.season, bf16[8,240,512]{2,1,0:T(8,128)(2,1)} %bitcast.10, f32[7,512]{1,0:T(8,128)} %bias.19, ...), custom_call_target="tpu_custom_call" | custom-call | flops 24999999488 | bytes 60000000 | tf_op jit(solution)/shard_map/up_grad_all/pallas_call | solution.py:98
  647.1 60.5 %tile_grad.1 = (f32[30,512,512]{2,1,0:T(8,128)}, f32[7,512]{1,0:T(8,128)}, f32[2,512]{1,0:T(2,128)}) custom-call(s32[1]{0:T(128)} %bitcast.2.sid.refs_0_, bf16[8,240,512]{2,1,0:T(8,128)(2,1)} %bitcast.11, bf16[8,256,512]{2,1,0:T(8,128)(2,1)} %bitcast.7, bf16[12,512,1024]{2,1,0:T(8,128)(2,1)} %get-tuple-element.139.flip_a, ...), custom_call_target="tpu_custom_call" | custom-call | flops 12999999488 | bytes 60000000 | tf_op jit(solution)/shard_map/tile_grad/pallas_call | solution.py:98
  (239 shorter events, 56.2 us)
Async XLA Ops:
  8.0 254.0 %all-gather.10.cloned.1.call-start = ((), (), s32[]{:S(2)}) async-start(), calls=%async_computation.3 | async-start | bytes 2211840 | tf_op jit(solution)/shard_map/all_gather | solution.py:933
  10.7 5.2 copy-start.27
  15.3 9.9 %collective-permute-start = (bf16[224,512]{1,0:T(8,128)(2,1)}, bf16[224,512]{1,0:T(8,128)(2,1)S(1)}, u32[]{:S(2)}, u32[]{:S(2)}) collective-permute-start(bf16[224,512]{1,0:T(8,128)(2,1)} %get-tuple-element.88), channel_id=1, source_target_pairs={{0,8},{1,9},{2,10},{3,11},{4,12},{5,13},{6,14},{7,15}} | collective-permute-start | bytes 688136 | tf_op jit(solution)/shard_map/ppermute | solution.py:878
  25.2 4.4 copy-start
  28.3 14.8 %collective-permute-start.1 = (bf16[224,512]{1,0:T(8,128)(2,1)}, bf16[224,512]{1,0:T(8,128)(2,1)S(1)}, u32[]{:S(2)}, u32[]{:S(2)}) collective-permute-start(bf16[224,512]{1,0:T(8,128)(2,1)} %get-tuple-element.89), channel_id=1, source_target_pairs={{8,16},{9,17},{10,18},{11,19},{12,20},{13,21},{14,22},{15,23}} | collective-permute-start | bytes 688136 | tf_op jit(solution)/shard_map/ppermute | solution.py:878
  59.5 7.2 %copy-start.2 = (bf16[224,512]{1,0:T(8,128)(2,1)S(1)}, bf16[224,512]{1,0:T(8,128)(2,1)}, u32[]{:S(2)}) copy-start(bf16[224,512]{1,0:T(8,128)(2,1)} %copy-done.1) | copy-start | bytes 688132
  59.5 7.2 %copy-start.12 = (bf16[224,512]{1,0:T(8,128)(2,1)S(1)}, bf16[224,512]{1,0:T(8,128)(2,1)}, u32[]{:S(2)}) copy-start(bf16[224,512]{1,0:T(8,128)(2,1)} %copy-done.11) | copy-start | bytes 688132
  61.0 10.5 %collective-permute-start.2 = (bf16[384,512]{1,0:T(8,128)(2,1)S(1)}, bf16[384,512]{1,0:T(8,128)(2,1)S(1)}, u32[]{:S(2)}, u32[]{:S(2)}) collective-permute-start(bf16[384,512]{1,0:T(8,128)(2,1)S(1)} %get-tuple-element.161), channel_id=1, source_target_pairs={{16,24},{17,25},{18,26},{19,27},{20,28},{21,29},{22,30},{23,31}} | collective-permute-start | bytes 1179656 | tf_op jit(solution)/shard_map/ppermute | solution.py:878
  67.5 206.4 %reduce-scatter.4.cloned.1.call-start = ((), (), s32[]{:S(2)}) async-start(), calls=%async_computation.6 | async-start | bytes 1966080
  67.5 34.7 %collective-permute-start.5 = (bf16[384,512]{1,0:T(8,128)(2,1)S(1)}, bf16[384,512]{1,0:T(8,128)(2,1)S(1)}, u32[]{:S(2)}, u32[]{:S(2)}) collective-permute-start(bf16[384,512]{1,0:T(8,128)(2,1)S(1)} %get-tuple-element.158), channel_id=1, source_target_pairs={{16,24},{17,25},{18,26},{19,27},{20,28},{21,29},{22,30},{23,31}} | collective-permute-start | bytes 1179656 | tf_op jit(solution)/shard_map/ppermute | solution.py:878
  68.8 29.7 %collective-permute-start.4 = (bf16[384,512]{1,0:T(8,128)(2,1)S(1)}, bf16[384,512]{1,0:T(8,128)(2,1)S(1)}, u32[]{:S(2)}, u32[]{:S(2)}) collective-permute-start(bf16[384,512]{1,0:T(8,128)(2,1)S(1)} %get-tuple-element.159), channel_id=1, source_target_pairs={{16,24},{17,25},{18,26},{19,27},{20,28},{21,29},{22,30},{23,31}} | collective-permute-start | bytes 1179656 | tf_op jit(solution)/shard_map/ppermute | solution.py:878
  70.2 24.9 %collective-permute-start.3 = (bf16[384,512]{1,0:T(8,128)(2,1)S(1)}, bf16[384,512]{1,0:T(8,128)(2,1)S(1)}, u32[]{:S(2)}, u32[]{:S(2)}) collective-permute-start(bf16[384,512]{1,0:T(8,128)(2,1)S(1)} %get-tuple-element.160), channel_id=1, source_target_pairs={{16,24},{17,25},{18,26},{19,27},{20,28},{21,29},{22,30},{23,31}} | collective-permute-start | bytes 1179656 | tf_op jit(solution)/shard_map/ppermute | solution.py:878
  74.2 31.6 %collective-permute-start.9 = (bf16[384,512]{1,0:T(8,128)(2,1)}, bf16[384,512]{1,0:T(8,128)(2,1)S(1)}, u32[]{:S(2)}, u32[]{:S(2)}) collective-permute-start(bf16[384,512]{1,0:T(8,128)(2,1)} %get-tuple-element.97), channel_id=1, source_target_pairs={{24,16},{25,17},{26,18},{27,19},{28,20},{29,21},{30,22},{31,23}} | collective-permute-start | bytes 1179656 | tf_op jit(solution)/shard_map/ppermute | solution.py:878
  97.3 20.7 %collective-permute-start.10 = (bf16[384,512]{1,0:T(8,128)(2,1)}, bf16[384,512]{1,0:T(8,128)(2,1)S(1)}, u32[]{:S(2)}, u32[]{:S(2)}) collective-permute-start(bf16[384,512]{1,0:T(8,128)(2,1)} %get-tuple-element.100), channel_id=1, source_target_pairs={{24,16},{25,17},{26,18},{27,19},{28,20},{29,21},{30,22},{31,23}} | collective-permute-start | bytes 1179656 | tf_op jit(solution)/shard_map/ppermute | solution.py:878
  100.9 30.2 %collective-permute-start.11 = (bf16[384,512]{1,0:T(8,128)(2,1)}, bf16[384,512]{1,0:T(8,128)(2,1)S(1)}, u32[]{:S(2)}, u32[]{:S(2)}) collective-permute-start(bf16[384,512]{1,0:T(8,128)(2,1)} %get-tuple-element.102), channel_id=1, source_target_pairs={{24,16},{25,17},{26,18},{27,19},{28,20},{29,21},{30,22},{31,23}} | collective-permute-start | bytes 1179656 | tf_op jit(solution)/shard_map/ppermute | solution.py:878
  104.4 39.6 %collective-permute-start.12 = (bf16[384,512]{1,0:T(8,128)(2,1)}, bf16[384,512]{1,0:T(8,128)(2,1)S(1)}, u32[]{:S(2)}, u32[]{:S(2)}) collective-permute-start(bf16[384,512]{1,0:T(8,128)(2,1)} %get-tuple-element.104), channel_id=1, source_target_pairs={{24,16},{25,17},{26,18},{27,19},{28,20},{29,21},{30,22},{31,23}} | collective-permute-start | bytes 1179656 | tf_op jit(solution)/shard_map/ppermute | solution.py:878
  161.0 4.6 collective-permute-start.13
  168.6 9.7 %collective-permute-start.14 = (bf16[224,512]{1,0:T(8,128)(2,1)}, bf16[224,512]{1,0:T(8,128)(2,1)S(1)}, u32[]{:S(2)}, u32[]{:S(2)}) collective-permute-start(bf16[224,512]{1,0:T(8,128)(2,1)} %get-tuple-element.107), channel_id=1, source_target_pairs={{8,0},{9,1},{10,2},{11,3},{12,4},{13,5},{14,6},{15,7}} | collective-permute-start | bytes 688136 | tf_op jit(solution)/shard_map/ppermute | solution.py:878
  169.3 8.4 %copy-start.22 = (f32[16,512]{1,0:T(8,128)S(1)}, f32[16,512]{1,0:T(8,128)}, u32[]{:S(2)}) copy-start(f32[16,512]{1,0:T(8,128)} %get-tuple-element.111) | copy-start | bytes 98308
  169.3 8.4 %copy-start.23 = (f32[16,512]{1,0:T(8,128)S(1)}, f32[16,512]{1,0:T(8,128)}, u32[]{:S(2)}) copy-start(f32[16,512]{1,0:T(8,128)} %get-tuple-element.112) | copy-start | bytes 98308
  169.3 8.4 %copy-start.24 = (f32[16,512]{1,0:T(8,128)S(1)}, f32[16,512]{1,0:T(8,128)}, u32[]{:S(2)}) copy-start(f32[16,512]{1,0:T(8,128)} %get-tuple-element.113) | copy-start | bytes 98308
  169.3 8.4 %copy-start.26 = (f32[16,512]{1,0:T(8,128)S(1)}, f32[16,512]{1,0:T(8,128)}, u32[]{:S(2)}) copy-start(f32[16,512]{1,0:T(8,128)} %get-tuple-element.114) | copy-start | bytes 98308
  233.9 1.2 copy-start.8
  233.9 1.3 copy-start.10
  234.0 121.4 %all-gather.8.cloned.1.call-start = ((), (), s32[]{:S(2)}) async-start(), calls=%async_computation.1 | async-start | bytes 14155776 | tf_op jit(solution)/shard_map/all_gather | solution.py:894
  234.7 237.3 %all-gather.14.cloned.1.call-start = ((), (), s32[]{:S(2)}) async-start(), calls=%async_computation.5 | async-start | bytes 14155776 | tf_op jit(solution)/shard_map/all_gather | solution.py:1048
  236.6 410.5 %all-reduce.9.cloned.1.call-start = ((), (), s32[]{:S(2)}) async-start(), calls=%async_computation.2 | async-start | bytes 9437184 | tf_op jit(solution)/shard_map/psum | solution.py:1069
  237.2 1.2 copy-start.16
  237.2 410.0 %all-gather.12.cloned.1.call-start = ((), (), s32[]{:S(2)}) async-start(), calls=%async_computation.4 | async-start | bytes 2359296 | tf_op jit(solution)/shard_map/all_gather | solution.py:1096
  238.6 3.5 collective-permute-start.6
  239.3 20.9 %collective-permute-start.8 = (bf16[1536,128]{1,0:T(8,128)(2,1)S(1)}, bf16[1536,128]{1,0:T(8,128)(2,1)S(1)}, u32[]{:S(2)}, u32[]{:S(2)}) collective-permute-start(bf16[1536,128]{1,0:T(8,128)(2,1)S(1)} %get-tuple-element.152), channel_id=1, source_target_pairs={{24,16},{25,17},{26,18},{27,19},{28,20},{29,21},{30,22},{31,23}} | collective-permute-start | bytes 1179656 | tf_op jit(solution)/shard_map/ppermute | solution.py:878
  240.6 19.6 %collective-permute-start.7 = (bf16[1536,128]{1,0:T(8,128)(2,1)S(1)}, bf16[1536,128]{1,0:T(8,128)(2,1)}, u32[]{:S(2)}, u32[]{:S(2)}) collective-permute-start(bf16[1536,128]{1,0:T(8,128)(2,1)S(1)} %get-tuple-element.153), channel_id=1, source_target_pairs={{24,8},{25,9},{26,10},{27,11},{28,12},{29,13},{30,14},{31,15}} | collective-permute-start | bytes 1179656 | tf_op jit(solution)/shard_map/ppermute | solution.py:878
  (21 other events, 17.2 us)
Sparse Core Ops, SparseCore 0:
  67.6 29.4 all-gather.9
  236.5 118.8 all-gather.7
  357.0 114.9 all-gather.13
  474.8 104.1 all-reduce.8
  580.4 29.6 all-gather.11
Sparse Core Ops, SparseCore 1:
  234.0 39.8 reduce-scatter.3
